TPU v7x, 512 devices: a whole 4x8x8 slice. The times are simulated.
512 devices in a mesh: phase: 32 (over y, x), tp: 8 (over z_lo, core), dp: 2 (over z_hi).
Axes of the slice: x: 4, y: 8, z: 8 (z_hi: 2, z_lo: 4; z = z_hi * 4 + z_lo), core: 2. Of those that a mesh axis runs over, the one named last changes fastest.
Arguments:
- down_inputs: bfloat16 [2, 32, 128, 1280], P('dp', 'phase', None, 'tp'), may hold values from -6 to 6
- up_inputs: bfloat16 [2, 32, 128, 1280], P('dp', 'phase', None, 'tp'), may hold values from -6 to 6
- down_cot: bfloat16 [2, 32, 128, 1280], P('dp', 'phase', None, 'tp'), may hold values from -6 to 6
- up_cot: bfloat16 [2, 32, 128, 1280], P('dp', 'phase', None, 'tp'), may hold values from -6 to 6
- segment_ids: int32 [2, 2, 32, 128], P(None, 'dp'), may hold values from 0 to 3, never falling along the last dimension, each value on 1 to 64 neighbouring positions
- patch_rows: int32 [2, 2, 32, 128], P(None, 'dp'), may hold values from 0 to 31
- patch_cols: int32 [2, 2, 32, 128], P(None, 'dp'), may hold values from 0 to 31
- w_qkv: bfloat16 [32, 3, 1280, 1280], P('phase', None, 'tp'), may hold values from -0.15625 to 0.15625
- w_out: bfloat16 [32, 1280, 1280], P('phase', 'tp'), may hold values from -0.15625 to 0.15625
Outputs:
- down_input_grad: bfloat16 [2, 32, 128, 1280], P('dp', 'phase', None, 'tp')
- up_input_grad: bfloat16 [2, 32, 128, 1280], P('dp', 'phase', None, 'tp')
- grad_qkv: bfloat16 [32, 3, 1280, 1280], P('phase', None, 'tp')
- grad_out: bfloat16 [32, 1280, 1280], P('phase', 'tp')
All inputs are finite; a program needn't handle non-finite values.
Results may differ from a plain program's by a relative error of at most 0.023.
Values may be sent and summed in bfloat16 or wider, within the bound.
A program may use at most 64 MiB of HBM per device.

v0:
```python
import math

import jax
import jax.numpy as jnp
from jax import lax
from jax.sharding import PartitionSpec as P

HD = 80


def from_behind(x, axis, by):
    length = lax.axis_size(axis)
    pairs = [(i, i + by) for i in range(length) if 0 <= i + by < length]
    return lax.ppermute(x, axis, pairs)


def normalize(vectors):
    average = jnp.mean(vectors, axis=1, keepdims=True)
    centred = vectors - average
    spread = jnp.mean(centred * centred, axis=1, keepdims=True)
    return centred * lax.rsqrt(spread + 1e-06)


def rotate(vectors, patch_row, patch_col):
    quarter = vectors.shape[1] // 4
    frequency = 10000.0 ** (-jnp.arange(quarter, dtype=jnp.float32) / quarter)

    def turn_pair(section, position):
        angles = position.astype(jnp.float32)[:, None] * frequency[None, :]
        cosine = jnp.cos(angles)
        sine_part = jnp.sin(angles)
        left = section[:, :quarter]
        right = section[:, quarter:]
        return jnp.concatenate(
            [left * cosine - right * sine_part, left * sine_part + right * cosine], axis=1
        )

    return jnp.concatenate(
        [
            turn_pair(vectors[:, : 2 * quarter], patch_row),
            turn_pair(vectors[:, 2 * quarter :], patch_col),
        ],
        axis=1,
    )


def attend(query_raw, key_raw, value_raw, segments, patch_row, patch_col):
    queries = rotate(normalize(query_raw), patch_row, patch_col)
    key_rows = rotate(normalize(key_raw), patch_row, patch_col)
    scores = jnp.dot(queries, key_rows.T, precision=lax.Precision.HIGHEST) / math.sqrt(
        query_raw.shape[1]
    )
    same_segment = segments[:, None] == segments[None, :]
    raised = jnp.where(same_segment, jnp.exp(scores), jnp.zeros_like(scores))
    weights_soft = raised / jnp.sum(raised, axis=1, keepdims=True)
    return jnp.dot(weights_soft, value_raw, precision=lax.Precision.HIGHEST)


def attend_all(project, segments, patch_row, patch_col):
    row_count = project.shape[0]
    sections = project.reshape(row_count, 3, project.shape[1] // (3 * HD), HD)

    def one_head(query_raw, key_raw, value_raw):
        return attend(query_raw, key_raw, value_raw, segments, patch_row, patch_col)

    blended = jax.vmap(one_head, in_axes=1, out_axes=1)(
        sections[:, 0], sections[:, 1], sections[:, 2]
    )
    return blended.reshape(row_count, -1)


def pull_heads(project, grad_heads, segments, patch_row, patch_col):

    def core(values_in):
        return attend_all(values_in, segments, patch_row, patch_col)

    _, pullback = jax.vjp(core, project)
    return pullback(grad_heads)[0]


def select_row(table, index):
    return lax.dynamic_index_in_dim(table, index, 0, keepdims=False)


def flip_blocks(matrix, count):
    row_count = matrix.shape[0]
    blocks = matrix.reshape(row_count, count, matrix.shape[1] // count)
    return blocks[:, ::-1].reshape(row_count, matrix.shape[1])


def mirror_weights(weights):
    count = lax.axis_size("phase")
    w_project, w_output = weights
    model_width = w_project.shape[2]
    spread_out = (
        lax.all_to_all(
            w_project.reshape(-1, model_width), "phase", split_axis=1, concat_axis=1, tiled=True
        ),
        lax.all_to_all(w_output, "phase", split_axis=1, concat_axis=1, tiled=True),
    )
    flipped = (flip_blocks(spread_out[0], count), flip_blocks(spread_out[1], count))
    collected = (
        lax.all_to_all(flipped[0], "phase", split_axis=1, concat_axis=1, tiled=True),
        lax.all_to_all(flipped[1], "phase", split_axis=1, concat_axis=1, tiled=True),
    )
    return (collected[0].reshape(w_project.shape), collected[1])


def mirror_grads(grads):
    count = lax.axis_size("phase")
    grad_project, grad_output = grads
    model_width = grad_project.shape[2]
    spread_out = (
        lax.all_to_all(
            grad_project.reshape(-1, model_width), "phase", split_axis=1, concat_axis=1, tiled=True
        ),
        lax.all_to_all(grad_output, "phase", split_axis=1, concat_axis=1, tiled=True),
    )
    flipped = (flip_blocks(spread_out[0], count), flip_blocks(spread_out[1], count))
    collected = (
        lax.all_to_all(flipped[0], "phase", split_axis=1, concat_axis=1, tiled=True),
        lax.all_to_all(flipped[1], "phase", split_axis=1, concat_axis=1, tiled=True),
    )
    return (collected[0].reshape(grad_project.shape), collected[1])


def forward_layer(inputs, weights, metadata, want_outputs):
    full = (
        lax.all_gather(inputs[0], "tp", axis=1, tiled=True),
        lax.all_gather(inputs[1], "tp", axis=1, tiled=True),
    )
    projections = []
    heads = []
    for relay in range(2):
        w_project = weights[relay][0]
        flat_weight = w_project.reshape(-1, w_project.shape[2])
        project = jnp.einsum(
            "rd,cd->rc", full[relay], flat_weight, preferred_element_type=jnp.float32
        )
        projections.append(project)
        meta = metadata[relay]
        heads.append(attend_all(project, meta[0], meta[1], meta[2]).astype(jnp.bfloat16))
    outputs = None
    if want_outputs:
        partial_sums = (
            lax.psum_scatter(
                jnp.dot(heads[0], weights[0][1], preferred_element_type=jnp.float32).astype(
                    jnp.bfloat16
                ),
                "tp",
                scatter_dimension=1,
                tiled=True,
            ).astype(jnp.float32),
            lax.psum_scatter(
                jnp.dot(heads[1], weights[1][1], preferred_element_type=jnp.float32).astype(
                    jnp.bfloat16
                ),
                "tp",
                scatter_dimension=1,
                tiled=True,
            ).astype(jnp.float32),
        )
        outputs = tuple(
            (
                (inputs[relay].astype(jnp.float32) + partial_sums[relay]).astype(jnp.bfloat16)
                for relay in range(2)
            )
        )
    return (outputs, (full, projections, heads))


def backward_layer(grads_in, weights, metadata, stored):
    full, projections, heads = stored
    grads_full = (
        lax.all_gather(grads_in[0], "tp", axis=1, tiled=True),
        lax.all_gather(grads_in[1], "tp", axis=1, tiled=True),
    )
    grad_outputs = []
    grad_projects = []
    terms = []
    for relay in range(2):
        w_project, w_output = weights[relay]
        grad_outputs.append(
            jnp.einsum(
                "rh,rd->hd", heads[relay], grads_full[relay], preferred_element_type=jnp.float32
            )
        )
        grad_heads = jnp.einsum(
            "rd,hd->rh", grads_full[relay], w_output, preferred_element_type=jnp.float32
        )
        meta = metadata[relay]
        grad_project = pull_heads(projections[relay], grad_heads, meta[0], meta[1], meta[2]).astype(
            jnp.bfloat16
        )
        flat_weight = w_project.reshape(-1, w_project.shape[2])
        grad_projects.append(
            jnp.einsum(
                "rc,rd->cd", grad_project, full[relay], preferred_element_type=jnp.float32
            ).reshape(w_project.shape)
        )
        terms.append(
            jnp.einsum("rc,cd->rd", grad_project, flat_weight, preferred_element_type=jnp.float32)
        )
    summed = (
        lax.psum_scatter(
            terms[0].astype(jnp.bfloat16), "tp", scatter_dimension=1, tiled=True
        ).astype(jnp.float32),
        lax.psum_scatter(
            terms[1].astype(jnp.bfloat16), "tp", scatter_dimension=1, tiled=True
        ).astype(jnp.float32),
    )
    grad_inputs = tuple(
        (
            (grads_in[relay].astype(jnp.float32) + summed[relay]).astype(jnp.bfloat16)
            for relay in range(2)
        )
    )
    return (grad_inputs, tuple(grad_projects), tuple(grad_outputs))


def per_device(
    down_inputs, up_inputs, down_cot, up_cot, segment_ids, patch_rows, patch_cols, w_qkv, w_out
):
    phases = lax.axis_size("phase")
    position = lax.axis_index("phase")
    down_weights = (w_qkv[0], w_out[0])
    up_weights = mirror_weights(down_weights)
    up_first = (up_inputs[0, 0], up_cot[0, 0])
    up_step = -1
    weights = (down_weights, up_weights)

    def describe(relay, index):
        return (
            select_row(segment_ids[relay, 0], index),
            select_row(patch_rows[relay, 0], index),
            select_row(patch_cols[relay, 0], index),
        )

    below = jnp.maximum(position - 1, 0)
    after = jnp.minimum(position + 1, phases - 1)
    first_meta = (describe(0, position), describe(1, position))
    second_meta = (describe(0, below), describe(1, after))
    first_in = (down_inputs[0, 0], up_first[0])
    first_out, first_stored = forward_layer(first_in, weights, first_meta, True)
    second_in = (from_behind(first_out[0], "phase", 1), from_behind(first_out[1], "phase", up_step))
    _, second_stored = forward_layer(second_in, weights, second_meta, False)
    second_dx, second_gq, second_go = backward_layer(
        (down_cot[0, 0], up_first[1]), weights, second_meta, second_stored
    )
    first_grads = (
        from_behind(second_dx[0], "phase", -1),
        from_behind(second_dx[1], "phase", -up_step),
    )
    first_dx, first_gq, first_go = backward_layer(first_grads, weights, first_meta, first_stored)
    down_q = first_gq[0] + second_gq[0]
    down_o = first_go[0] + second_go[0]
    up_rounded = (
        (first_gq[1] + second_gq[1]).astype(jnp.bfloat16),
        (first_go[1] + second_go[1]).astype(jnp.bfloat16),
    )
    received = mirror_grads(up_rounded)
    up_grad_rows = first_dx[1]
    totals = (down_q + received[0].astype(jnp.float32), down_o + received[1].astype(jnp.float32))
    grad_q, grad_o = (
        lax.psum(totals[0].astype(jnp.bfloat16), "dp").astype(jnp.float32),
        lax.psum(totals[1].astype(jnp.bfloat16), "dp").astype(jnp.float32),
    )
    return (
        first_dx[0][None, None],
        up_grad_rows[None, None],
        grad_q.astype(jnp.bfloat16)[None],
        grad_o.astype(jnp.bfloat16)[None],
    )


def solution(mesh):
    return jax.shard_map(
        per_device,
        mesh=mesh,
        in_specs=(
            P("dp", "phase", None, "tp"),
            P("dp", "phase", None, "tp"),
            P("dp", "phase", None, "tp"),
            P("dp", "phase", None, "tp"),
            P(None, "dp", None, None),
            P(None, "dp", None, None),
            P(None, "dp", None, None),
            P("phase", None, "tp", None),
            P("phase", "tp", None),
        ),
        out_specs=(
            P("dp", "phase", None, "tp"),
            P("dp", "phase", None, "tp"),
            P("phase", None, "tp", None),
            P("phase", "tp", None),
        ),
        check_vma=False,
    )
```

profile of v0, /device:TPU:1, one launch (start us, length us, event | category | flops | bytes accessed | tf_op | source)
XLA Modules:
  0.0 672.3 jit_solution(6913332007416256104)
XLA Ops:
  7.3 21.2 %all-gather.1 = bf16[1,1,128,1280]{2,3,1,0:T(8,128)(2,1)S(1)} all-gather(bf16[1,1,128,160]{2,3,1,0:T(8,128)(2,1)} %param.9), channel_id=3, replica_groups=mesh['phase'=32,'tp'=8,'dp'=2] {'tp'}, dimensions={3}, use_global_device_ids=true | all-gather | bytes 368640 | tf_op jit(solution)/shard_map/all_gather | solution.py:129
  37.9 6.0 all_to_all.56
  44.0 7.1 %all-to-all-start.2 = ((bf16[480,32,40]{0,2,1:T(8,128)(2,1)}), bf16[480,32,40]{0,2,1:T(8,128)(2,1)}, u32[]{:S(2)}, u32[]{:S(2)}) async-start(bf16[480,32,40]{0,2,1:T(8,128)(2,1)} %all_to_all.56), calls=%async_computation.5 | async-start | bytes 2621440 | tf_op jit(solution)/shard_map/all_to_all | solution.py:96
  51.2 14.7 %all-gather = bf16[1,1,128,1280]{2,3,1,0:T(8,128)(2,1)S(1)} all-gather(bf16[1,1,128,160]{2,3,1,0:T(8,128)(2,1)S(1)} %copy-done.55), channel_id=2, replica_groups=mesh['phase'=32,'tp'=8,'dp'=2] {'tp'}, dimensions={3}, use_global_device_ids=true | all-gather | bytes 368640 | tf_op jit(solution)/shard_map/all_gather | solution.py:175
  66.0 15.6 %all-gather.3 = bf16[1,1,128,1280]{2,3,1,0:T(8,128)(2,1)} all-gather(bf16[1,1,128,160]{2,3,1,0:T(8,128)(2,1)S(1)} %copy-done.52), channel_id=5, replica_groups=mesh['phase'=32,'tp'=8,'dp'=2] {'tp'}, dimensions={3}, use_global_device_ids=true | all-gather | bytes 368640 | tf_op jit(solution)/shard_map/all_gather | solution.py:130
  88.0 15.7 %all-gather.2 = bf16[1,1,128,1280]{2,3,1,0:T(8,128)(2,1)} all-gather(bf16[1,1,128,160]{2,3,1,0:T(8,128)(2,1)S(1)} %copy-done.54), channel_id=4, replica_groups=mesh['phase'=32,'tp'=8,'dp'=2] {'tp'}, dimensions={3}, use_global_device_ids=true | all-gather | bytes 368640 | tf_op jit(solution)/shard_map/all_gather | solution.py:176
  104.7 14.3 %all_gather.26 = bf16[128,1280]{0,1:T(8,128)(2,1)S(1)} all-gather(bf16[128,160]{0,1:T(8,128)(2,1)S(1)} %collective-permute-done), channel_id=1, replica_groups=mesh['phase'=32,'tp'=8,'dp'=2] {'tp'}, dimensions={1}, use_global_device_ids=true | all-gather | bytes 368640 | tf_op jit(solution)/shard_map/all_gather | solution.py:129
  119.8 8.9 %all-to-all-start = ((bf16[160,32,40]{0,2,1:T(8,128)(2,1)}), bf16[160,32,40]{0,2,1:T(8,128)(2,1)S(1)}, u32[]{:S(2)}, u32[]{:S(2)}) async-start(bf16[160,32,40]{0,2,1:T(8,128)(2,1)} %bitcast.466), calls=%async_computation.3 | async-start | bytes 1310720 | tf_op jit(solution)/shard_map/all_to_all | solution.py:99
  132.0 15.8 %all-to-all-done = bf16[160,32,40]{0,2,1:T(8,128)(2,1)S(1)} async-done(((bf16[160,32,40]{0,2,1:T(8,128)(2,1)}), bf16[160,32,40]{0,2,1:T(8,128)(2,1)S(1)}, u32[]{:S(2)}, u32[]{:S(2)}) %all-to-all-start) | async-done | bytes 409632 | tf_op jit(solution)/shard_map/all_to_all | solution.py:99
  161.4 23.5 %all-to-all-done.3 = bf16[480,32,40]{0,2,1:T(8,128)(2,1)S(1)} async-done(((bf16[480,32,40]{0,2,1:T(8,128)(2,1)}), bf16[480,32,40]{0,2,1:T(8,128)(2,1)S(1)}, u32[]{:S(2)}, u32[]{:S(2)}) %all-to-all-start.3) | async-done | bytes 1228832 | tf_op jit(solution)/shard_map/all_to_all | solution.py:103
  184.9 7.1 %all-to-all-start.1 = ((bf16[160,32,40]{0,2,1:T(8,128)(2,1)}), bf16[160,32,40]{0,2,1:T(8,128)(2,1)}, u32[]{:S(2)}, u32[]{:S(2)}) async-start(bf16[160,32,40]{0,2,1:T(8,128)(2,1)} %all_to_all.54), calls=%async_computation.4 | async-start | bytes 1310720 | tf_op jit(solution)/shard_map/all_to_all | solution.py:104
  218.0 30.4 %reduce-scatter.13.cloned.1.call-done = bf16[128,160]{0,1:T(8,128)(2,1)} async-done(((bf16[128,1280]{0,1:T(8,128)(2,1)}), bf16[128,160]{0,1:T(8,128)(2,1)}) %reduce-scatter.13.cloned.1.call-update) | async-done | bytes 40976 | tf_op jit(solution)/shard_map/reduce_scatter | solution.py:154
  254.0 18.7 %all_gather.30 = bf16[128,1280]{0,1:T(8,128)(2,1)S(1)} all-gather(bf16[128,160]{0,1:T(8,128)(2,1)S(1)} %collective-permute-done.2), channel_id=1, replica_groups=mesh['phase'=32,'tp'=8,'dp'=2] {'tp'}, dimensions={1}, use_global_device_ids=true | all-gather | bytes 368640 | tf_op jit(solution)/shard_map/all_gather | solution.py:130
  284.1 30.1 %reduce-scatter.15.cloned.1.call-done = bf16[128,160]{0,1:T(8,128)(2,1)} async-done(((bf16[128,1280]{0,1:T(8,128)(2,1)}), bf16[128,160]{0,1:T(8,128)(2,1)}) %reduce-scatter.15.cloned.1.call-update) | async-done | bytes 40976 | tf_op jit(solution)/shard_map/reduce_scatter | solution.py:208
  319.4 19.3 %all_gather.31 = bf16[128,1280]{0,1:T(8,128)(2,1)S(1)} all-gather(bf16[128,160]{0,1:T(8,128)(2,1)S(1)} %collective-permute-done.3), channel_id=1, replica_groups=mesh['phase'=32,'tp'=8,'dp'=2] {'tp'}, dimensions={1}, use_global_device_ids=true | all-gather | bytes 368640 | tf_op jit(solution)/shard_map/all_gather | solution.py:176
  345.3 10.7 %all-to-all-start.6 = ((bf16[160,32,40]{0,2,1:T(8,128)(2,1)}), bf16[160,32,40]{0,2,1:T(8,128)(2,1)}, u32[]{:S(2)}, u32[]{:S(2)}) async-start(bf16[160,32,40]{0,2,1:T(8,128)(2,1)} %bitcast.467), calls=%async_computation.12 | async-start | bytes 1310720 | tf_op jit(solution)/shard_map/all_to_all | solution.py:117
  375.1 6.1 all-to-all-start.4
  389.0 15.0 %all_gather.27 = bf16[128,1280]{0,1:T(8,128)(2,1)S(1)} all-gather(bf16[128,160]{0,1:T(8,128)(2,1)S(1)} %collective-permute-done.1), channel_id=1, replica_groups=mesh['phase'=32,'tp'=8,'dp'=2] {'tp'}, dimensions={1}, use_global_device_ids=true | all-gather | bytes 368640 | tf_op jit(solution)/shard_map/all_gather | solution.py:175
  412.3 27.3 %all-to-all-start.7 = ((bf16[160,32,40]{0,2,1:T(8,128)(2,1)}), bf16[160,32,40]{0,2,1:T(8,128)(2,1)S(1)}, u32[]{:S(2)}, u32[]{:S(2)}) async-start(bf16[160,32,40]{0,2,1:T(8,128)(2,1)} %all_to_all.68), calls=%async_computation.13 | async-start | bytes 1310720 | tf_op jit(solution)/shard_map/all_to_all | solution.py:122
  444.8 13.8 %all-to-all-done.7 = bf16[160,32,40]{0,2,1:T(8,128)(2,1)S(1)} async-done(((bf16[160,32,40]{0,2,1:T(8,128)(2,1)}), bf16[160,32,40]{0,2,1:T(8,128)(2,1)S(1)}, u32[]{:S(2)}, u32[]{:S(2)}) %all-to-all-start.7) | async-done | bytes 409632 | tf_op jit(solution)/shard_map/all_to_all | solution.py:122
  477.3 18.6 %all-to-all-done.5 = bf16[480,32,40]{0,2,1:T(8,128)(2,1)} async-done(((bf16[480,32,40]{0,2,1:T(8,128)(2,1)}), bf16[480,32,40]{0,2,1:T(8,128)(2,1)}, u32[]{:S(2)}, u32[]{:S(2)}) %all-to-all-start.5) | async-done | bytes 1228832 | tf_op jit(solution)/shard_map/all_to_all | solution.py:121
  495.9 6.9 %reshape.866 = f32[3,160,1280]{1,0,2:T(4,128)} reshape(bf16[480,32,40]{0,2,1:T(8,128)(2,1)} %all-to-all-done.5) | data formatting | bytes 3686400 | tf_op jit(solution)/shard_map/convert_element_type | solution.py:263
  514.2 32.7 %reduce-scatter.17.cloned.1.call-done = bf16[128,160]{0,1:T(8,128)(2,1)} async-done(((bf16[128,1280]{0,1:T(8,128)(2,1)}), bf16[128,160]{0,1:T(8,128)(2,1)}) %reduce-scatter.17.cloned.1.call-update) | async-done | bytes 40976 | tf_op jit(solution)/shard_map/reduce_scatter | solution.py:208
  548.3 113.9 %all-reduce.63.cloned.1.call-done = (bf16[1,3,160,1280]{3,2,1,0:T(8,128)(2,1)}, bf16[1,160,1280]{2,1,0:T(8,128)(2,1)}) async-done(((bf16[1,3,160,1280]{3,2,1,0:T(8,128)(2,1)}, bf16[1,160,1280]{2,1,0:T(8,128)(2,1)}), (bf16[1,3,160,1280]{3,2,1,0:T(8,128)(2,1)}, bf16[1,160,1280]{2,1,0:T(8,128)(2,1)})) %all-reduce.63.cloned.1.call-update) | async-done | bytes 1638416 | tf_op jit(solution)/shard_map/psum | solution.py:265
  (545 shorter events, 162.0 us)
Async XLA Ops:
  7.2 76.7 %reduce-scatter.7.cloned.1.call-start = ((), (), s32[]{:S(2)}) async-start(), calls=%async_computation.14 | async-start | bytes 368640 | tf_op jit(solution)/shard_map/reduce_scatter | solution.py:146
  32.4 171.4 %copy-start.37 = (f32[128,20]{0,1:T(8,128)}, f32[128,20]{0,1:T(8,128)S(1)}, u32[]{:S(2)}) copy-start(f32[128,20]{0,1:T(8,128)S(1)} %get-tuple-element.190) | copy-start | bytes 30724
  32.4 171.4 %copy-start.39 = (f32[128,20]{0,1:T(8,128)}, f32[128,20]{0,1:T(8,128)S(1)}, u32[]{:S(2)}) copy-start(f32[128,20]{0,1:T(8,128)S(1)} %get-tuple-element.191) | copy-start | bytes 30724
  32.4 171.4 %copy-start.41 = (f32[128,20]{0,1:T(8,128)}, f32[128,20]{0,1:T(8,128)S(1)}, u32[]{:S(2)}) copy-start(f32[128,20]{0,1:T(8,128)S(1)} %get-tuple-element.192) | copy-start | bytes 30724
  32.4 171.4 %copy-start.43 = (f32[128,20]{0,1:T(8,128)}, f32[128,20]{0,1:T(8,128)S(1)}, u32[]{:S(2)}) copy-start(f32[128,20]{0,1:T(8,128)S(1)} %get-tuple-element.193) | copy-start | bytes 30724
  44.0 75.7 %all-to-all-start.2 = ((bf16[480,32,40]{0,2,1:T(8,128)(2,1)}), bf16[480,32,40]{0,2,1:T(8,128)(2,1)}, u32[]{:S(2)}, u32[]{:S(2)}) async-start(bf16[480,32,40]{0,2,1:T(8,128)(2,1)} %all_to_all.56), calls=%async_computation.5 | async-start | bytes 2621440 | tf_op jit(solution)/shard_map/all_to_all | solution.py:96
  51.2 104.6 %copy-start.73 = (pred[128,128]{0,1:T(8,128)(4,1)}, pred[128,128]{0,1:T(8,128)(4,1)S(1)}, u32[]{:S(2)}) copy-start(pred[128,128]{0,1:T(8,128)(4,1)S(1)} %broadcast_compare_fusion.3) | copy-start | bytes 49156
  84.7 20.0 %collective-permute-start = (bf16[128,160]{0,1:T(8,128)(2,1)S(1)}, bf16[128,160]{0,1:T(8,128)(2,1)S(1)}, u32[]{:S(2)}, u32[]{:S(2)}) collective-permute-start(bf16[128,160]{0,1:T(8,128)(2,1)S(1)} %fusion.37), channel_id=1, source_target_pairs={{0,16},{16,32},{32,48},{48,64},{64,80},{80,96},{96,112},{112,128},... | collective-permute-start | bytes 122888 | tf_op jit(solution)/shard_map/ppermute | solution.py:14
  119.8 27.9 %all-to-all-start = ((bf16[160,32,40]{0,2,1:T(8,128)(2,1)}), bf16[160,32,40]{0,2,1:T(8,128)(2,1)S(1)}, u32[]{:S(2)}, u32[]{:S(2)}) async-start(bf16[160,32,40]{0,2,1:T(8,128)(2,1)} %bitcast.466), calls=%async_computation.3 | async-start | bytes 1310720 | tf_op jit(solution)/shard_map/all_to_all | solution.py:99
  148.6 36.3 %all-to-all-start.3 = ((bf16[480,32,40]{0,2,1:T(8,128)(2,1)}), bf16[480,32,40]{0,2,1:T(8,128)(2,1)S(1)}, u32[]{:S(2)}, u32[]{:S(2)}) async-start(bf16[480,32,40]{0,2,1:T(8,128)(2,1)} %all_to_all.58), calls=%async_computation.6 | async-start | bytes 2621440 | tf_op jit(solution)/shard_map/all_to_all | solution.py:103
  184.9 24.0 %all-to-all-start.1 = ((bf16[160,32,40]{0,2,1:T(8,128)(2,1)}), bf16[160,32,40]{0,2,1:T(8,128)(2,1)}, u32[]{:S(2)}, u32[]{:S(2)}) async-start(bf16[160,32,40]{0,2,1:T(8,128)(2,1)} %all_to_all.54), calls=%async_computation.4 | async-start | bytes 1310720 | tf_op jit(solution)/shard_map/all_to_all | solution.py:104
  192.0 56.4 %reduce-scatter.13.cloned.1.call-start = ((), (), s32[]{:S(2)}) async-start(), calls=%async_computation.17 | async-start | bytes 368640 | tf_op jit(solution)/shard_map/reduce_scatter | solution.py:154
  211.0 103.2 %reduce-scatter.15.cloned.1.call-start = ((), (), s32[]{:S(2)}) async-start(), calls=%async_computation.18 | async-start | bytes 368640 | tf_op jit(solution)/shard_map/reduce_scatter | solution.py:208
  249.3 4.7 collective-permute-start.2
  277.9 103.4 %reduce-scatter.9.cloned.1.call-start = ((), (), s32[]{:S(2)}) async-start(), calls=%async_computation.15 | async-start | bytes 368640 | tf_op jit(solution)/shard_map/reduce_scatter | solution.py:205
  315.0 3.7 collective-permute-start.3
  345.3 29.8 %all-to-all-start.6 = ((bf16[160,32,40]{0,2,1:T(8,128)(2,1)}), bf16[160,32,40]{0,2,1:T(8,128)(2,1)}, u32[]{:S(2)}, u32[]{:S(2)}) async-start(bf16[160,32,40]{0,2,1:T(8,128)(2,1)} %bitcast.467), calls=%async_computation.12 | async-start | bytes 1310720 | tf_op jit(solution)/shard_map/all_to_all | solution.py:117
  375.1 37.2 %all-to-all-start.4 = ((bf16[480,32,40]{0,2,1:T(8,128)(2,1)}), bf16[480,32,40]{0,2,1:T(8,128)(2,1)}, u32[]{:S(2)}, u32[]{:S(2)}) async-start(bf16[480,32,40]{0,2,1:T(8,128)(2,1)} %all_to_all.62), calls=%async_computation.10 | async-start | bytes 2621440 | tf_op jit(solution)/shard_map/all_to_all | solution.py:114
  382.2 6.8 %collective-permute-start.1 = (bf16[128,160]{0,1:T(8,128)(2,1)S(1)}, bf16[128,160]{0,1:T(8,128)(2,1)S(1)}, u32[]{:S(2)}, u32[]{:S(2)}) collective-permute-start(bf16[128,160]{0,1:T(8,128)(2,1)S(1)} %fusion.38), channel_id=1, source_target_pairs={{16,0},{32,16},{48,32},{64,48},{80,64},{96,80},{112,96},{128,112},... | collective-permute-start | bytes 122888 | tf_op jit(solution)/shard_map/ppermute | solution.py:14
  412.3 46.3 %all-to-all-start.7 = ((bf16[160,32,40]{0,2,1:T(8,128)(2,1)}), bf16[160,32,40]{0,2,1:T(8,128)(2,1)S(1)}, u32[]{:S(2)}, u32[]{:S(2)}) async-start(bf16[160,32,40]{0,2,1:T(8,128)(2,1)} %all_to_all.68), calls=%async_computation.13 | async-start | bytes 1310720 | tf_op jit(solution)/shard_map/all_to_all | solution.py:122
  459.4 36.4 %all-to-all-start.5 = ((bf16[480,32,40]{0,2,1:T(8,128)(2,1)}), bf16[480,32,40]{0,2,1:T(8,128)(2,1)}, u32[]{:S(2)}, u32[]{:S(2)}) async-start(bf16[480,32,40]{0,2,1:T(8,128)(2,1)} %all_to_all.64), calls=%async_computation.11 | async-start | bytes 2621440 | tf_op jit(solution)/shard_map/all_to_all | solution.py:121
  465.0 47.0 %reduce-scatter.11.cloned.1.call-start = ((), (), s32[]{:S(2)}) async-start(), calls=%async_computation.16 | async-start | bytes 368640 | tf_op jit(solution)/shard_map/reduce_scatter | solution.py:205
  469.4 77.5 %reduce-scatter.17.cloned.1.call-start = ((), (), s32[]{:S(2)}) async-start(), calls=%async_computation.19 | async-start | bytes 368640 | tf_op jit(solution)/shard_map/reduce_scatter | solution.py:208
  474.1 188.2 %all-reduce.63.cloned.1.call-start = ((), (), s32[]{:S(2)}) async-start(), calls=%async_computation.20 | async-start | bytes 3276800 | tf_op jit(solution)/shard_map/psum | solution.py:265
  (162 other events, 1786.8 us)
Sparse Core Ops, SparseCore 0:
  34.7 35.6 reduce-scatter.6
  211.1 37.1 reduce-scatter.12
  278.0 36.1 reduce-scatter.14
  317.0 37.5 reduce-scatter.8
  469.5 37.1 reduce-scatter.10
  509.6 37.1 reduce-scatter.16
  550.4 111.7 all-reduce.62
where the time goes:
time: 676 us; the launch traced here: 672 us
  waiting for transfers between devices  295 us (44%)
  blocking collectives  134 us (20%)
  starting transfers between devices  86.9 us (13%)
  local copies, waits for them, and re-layouts  71.2 us (11%)
  matrix products  43.9 us (6%)
  other arithmetic  23.4 us (3%)
  between operations  16.9 us (2%)
    psum x1, waiting for transfers between devices, per_device(): lax.psum(totals[0].astype(jnp.bfloat16), 'dp').astype(jnp.float32)  114 us
    reduce_scatter x2, waiting for transfers between devices, backward_layer(): lax.psum_scatter(terms[1].astype(jnp.bfloat16), 'tp', scatter_dimension=1...  62.7 us
    all_gather x2, blocking collectives, forward_layer(): lax.all_gather(inputs[0], 'tp', axis=1, tiled=True)  35.5 us
    all_gather x2, blocking collectives, backward_layer(): lax.all_gather(grads_in[1], 'tp', axis=1, tiled=True)  35 us
    all_gather x2, blocking collectives, forward_layer(): lax.all_gather(inputs[1], 'tp', axis=1, tiled=True)  34.3 us
    reduce_scatter x1, waiting for transfers between devices, forward_layer(): lax.psum_scatter(jnp.dot(heads[1], weights[1][1], preferred_element_type=...  30.4 us
    all_gather x2, blocking collectives, backward_layer(): lax.all_gather(grads_in[0], 'tp', axis=1, tiled=True)  29.7 us
    all_to_all x1, starting transfers between devices, mirror_grads(): lax.all_to_all(flipped[1], 'phase', split_axis=1, concat_axis=1, tiled=True)  27.3 us
  transfers between devices with their start and end apart: 19, of which 13 were waited for; matrix products, arithmetic and copies ran while one was open for 14% of the time, Pallas kernels for 0%

commit v1 on v0

v1 whole, which is shorter than its diff:
```python
import math

import jax
import jax.numpy as jnp
from jax import lax
from jax.sharding import PartitionSpec as P

HD = 80


def from_behind(x, axis, by):
    length = lax.axis_size(axis)
    pairs = [(i, i + by) for i in range(length) if 0 <= i + by < length]
    return lax.ppermute(x, axis, pairs)


def normalize(vectors):
    average = jnp.mean(vectors, axis=1, keepdims=True)
    centred = vectors - average
    spread = jnp.mean(centred * centred, axis=1, keepdims=True)
    return centred * lax.rsqrt(spread + 1e-06)


def rotate(vectors, patch_row, patch_col):
    quarter = vectors.shape[1] // 4
    frequency = 10000.0 ** (-jnp.arange(quarter, dtype=jnp.float32) / quarter)

    def turn_pair(section, position):
        angles = position.astype(jnp.float32)[:, None] * frequency[None, :]
        cosine = jnp.cos(angles)
        sine_part = jnp.sin(angles)
        left = section[:, :quarter]
        right = section[:, quarter:]
        return jnp.concatenate(
            [left * cosine - right * sine_part, left * sine_part + right * cosine], axis=1
        )

    return jnp.concatenate(
        [
            turn_pair(vectors[:, : 2 * quarter], patch_row),
            turn_pair(vectors[:, 2 * quarter :], patch_col),
        ],
        axis=1,
    )


def attend(query_raw, key_raw, value_raw, segments, patch_row, patch_col):
    queries = rotate(normalize(query_raw), patch_row, patch_col)
    key_rows = rotate(normalize(key_raw), patch_row, patch_col)
    scores = jnp.dot(queries, key_rows.T, precision=lax.Precision.HIGHEST) / math.sqrt(
        query_raw.shape[1]
    )
    same_segment = segments[:, None] == segments[None, :]
    raised = jnp.where(same_segment, jnp.exp(scores), jnp.zeros_like(scores))
    weights_soft = raised / jnp.sum(raised, axis=1, keepdims=True)
    return jnp.dot(weights_soft, value_raw, precision=lax.Precision.HIGHEST)


def attend_all(project, segments, patch_row, patch_col):
    row_count = project.shape[0]
    sections = project.reshape(row_count, 3, project.shape[1] // (3 * HD), HD)

    def one_head(query_raw, key_raw, value_raw):
        return attend(query_raw, key_raw, value_raw, segments, patch_row, patch_col)

    blended = jax.vmap(one_head, in_axes=1, out_axes=1)(
        sections[:, 0], sections[:, 1], sections[:, 2]
    )
    return blended.reshape(row_count, -1)


def pull_heads(project, grad_heads, segments, patch_row, patch_col):

    def core(values_in):
        return attend_all(values_in, segments, patch_row, patch_col)

    _, pullback = jax.vjp(core, project)
    return pullback(grad_heads)[0]


def select_row(table, index):
    return lax.dynamic_index_in_dim(table, index, 0, keepdims=False)


def forward_layer(inputs, w_project, w_output, metadata, want_outputs):
    full = lax.all_gather(inputs, "tp", axis=2, tiled=True)
    flat_weight = w_project.reshape(-1, w_project.shape[2])
    project = jnp.einsum("brd,cd->brc", full, flat_weight, preferred_element_type=jnp.float32)
    heads = jax.vmap(attend_all)(project, *metadata).astype(jnp.bfloat16)
    outputs = None
    if want_outputs:
        term = jnp.einsum("brh,hd->brd", heads, w_output, preferred_element_type=jnp.float32)
        summed = lax.psum_scatter(
            term.astype(jnp.bfloat16), "tp", scatter_dimension=2, tiled=True
        )
        outputs = (inputs.astype(jnp.float32) + summed.astype(jnp.float32)).astype(jnp.bfloat16)
    return outputs, (full, project, heads)


def backward_layer(grads_in, w_project, w_output, metadata, stored):
    full, project, heads = stored
    grads_full = lax.all_gather(grads_in, "tp", axis=2, tiled=True)
    grad_output = jnp.einsum("brh,brd->hd", heads, grads_full, preferred_element_type=jnp.float32)
    grad_heads = jnp.einsum("brd,hd->brh", grads_full, w_output, preferred_element_type=jnp.float32)
    grad_project = jax.vmap(pull_heads)(project, grad_heads, *metadata).astype(jnp.bfloat16)
    flat_weight = w_project.reshape(-1, w_project.shape[2])
    grad_weight = jnp.einsum("brc,brd->cd", grad_project, full, preferred_element_type=jnp.float32)
    term = jnp.einsum("brc,cd->brd", grad_project, flat_weight, preferred_element_type=jnp.float32)
    summed = lax.psum_scatter(term.astype(jnp.bfloat16), "tp", scatter_dimension=2, tiled=True)
    grad_inputs = (grads_in.astype(jnp.float32) + summed.astype(jnp.float32)).astype(jnp.bfloat16)
    return grad_inputs, grad_weight, grad_output


def mirror(x):
    count = lax.axis_size("phase")
    return lax.ppermute(x, "phase", [(i, count - 1 - i) for i in range(count)])


def per_device(
    down_inputs, up_inputs, down_cot, up_cot, segment_ids, patch_rows, patch_cols, w_qkv, w_out
):
    phases = lax.axis_size("phase")
    position = lax.axis_index("phase")
    mirrored = mirror(jnp.stack([up_inputs[0, 0], up_cot[0, 0]]))
    first_in = jnp.stack([down_inputs[0, 0], mirrored[0]])
    last_cot = jnp.stack([down_cot[0, 0], mirrored[1]])
    w_project, w_output = w_qkv[0], w_out[0]

    def describe(index):
        other = phases - 1 - index
        return tuple(
            jnp.stack([select_row(table[0, 0], index), select_row(table[1, 0], other)])
            for table in (segment_ids, patch_rows, patch_cols)
        )

    first_meta = describe(position)
    second_meta = describe(jnp.maximum(position - 1, 0))
    first_out, first_stored = forward_layer(first_in, w_project, w_output, first_meta, True)
    second_in = from_behind(first_out, "phase", 1)
    _, second_stored = forward_layer(second_in, w_project, w_output, second_meta, False)
    second_dx, second_gq, second_go = backward_layer(
        last_cot, w_project, w_output, second_meta, second_stored
    )
    first_grads = from_behind(second_dx, "phase", -1)
    first_dx, first_gq, first_go = backward_layer(
        first_grads, w_project, w_output, first_meta, first_stored
    )
    total = jnp.concatenate([first_gq + second_gq, first_go + second_go]).astype(jnp.bfloat16)
    other = lax.ppermute(total, "dp", [(0, 1), (1, 0)])
    both = (total.astype(jnp.float32) + other.astype(jnp.float32)).astype(jnp.bfloat16)
    rows = w_project.shape[0] * w_project.shape[1]
    return (
        first_dx[0][None, None],
        mirror(first_dx[1])[None, None],
        both[:rows].reshape(w_qkv.shape),
        both[rows:].reshape(w_out.shape),
    )


def solution(mesh):
    return jax.shard_map(
        per_device,
        mesh=mesh,
        in_specs=(
            P("dp", "phase", None, "tp"),
            P("dp", "phase", None, "tp"),
            P("dp", "phase", None, "tp"),
            P("dp", "phase", None, "tp"),
            P(None, "dp", None, None),
            P(None, "dp", None, None),
            P(None, "dp", None, None),
            P("phase", None, "tp", None),
            P("phase", "tp", None),
        ),
        out_specs=(
            P("dp", "phase", None, "tp"),
            P("dp", "phase", None, "tp"),
            P("phase", None, "tp", None),
            P("phase", "tp", None),
        ),
        check_vma=False,
    )
```

time: 676 us -> 296 us (0.44)
  the two profiles are of different devices: /device:TPU:1 before, /device:TPU:150 now
where the time goes in v1:
time: 296 us; the launch traced here: 295 us
  waiting for transfers between devices  146 us (49%)
  blocking collectives  68.2 us (23%)
  starting transfers between devices  22.2 us (8%)
  matrix products  22.1 us (7%)
  between operations  14.9 us (5%)
  other arithmetic  12.8 us (4%)
  local copies, waits for them, and re-layouts  9.09 us (3%)
    reduce_scatter x2, waiting for transfers between devices, backward_layer(): lax.psum_scatter(term.astype(jnp.bfloat16), 'tp', scatter_dimension=2, ti...  112 us
    all_gather x2, blocking collectives, backward_layer(): grads_full = lax.all_gather(grads_in, 'tp', axis=2, tiled=True)  34.8 us
    all_gather x2, blocking collectives, forward_layer(): full = lax.all_gather(inputs, 'tp', axis=2, tiled=True)  33.5 us
    reduce_scatter x1, waiting for transfers between devices, forward_layer(): lax.psum_scatter(term.astype(jnp.bfloat16), 'tp', scatter_dimension=2, ti...  20.3 us
    ppermute x2, starting transfers between devices, mirror(): return lax.ppermute(x, 'phase', [(i, count - 1 - i) for i in range(count)])  11.1 us
    ppermute x2, waiting for transfers between devices, from_behind(): return lax.ppermute(x, axis, pairs)  6.95 us
    ppermute x2, waiting for transfers between devices, mirror(): return lax.ppermute(x, 'phase', [(i, count - 1 - i) for i in range(count)])  6.7 us
    ppermute x2, starting transfers between devices, from_behind(): return lax.ppermute(x, axis, pairs)  6.12 us
  transfers between devices with their start and end apart: 8, of which 7 were waited for; matrix products, arithmetic and copies ran while one was open for 6% of the time, Pallas kernels for 0%

profile of v1, /device:TPU:150, one launch (start us, length us, event | category | flops | bytes accessed | tf_op | source)
XLA Modules:
  0.0 295.5 jit_solution(9826063423119424537)
XLA Ops:
  8.1 5.7 %collective-permute-start = (bf16[2,128,160]{1,2,0:T(8,128)(2,1)S(1)}, bf16[2,128,160]{1,2,0:T(8,128)(2,1)S(1)}, u32[]{:S(2)}, u32[]{:S(2)}) collective-permute-start(bf16[2,128,160]{1,2,0:T(8,128)(2,1)S(1)} %pad_maximum_fusion.5), channel_id=1, source_target_pairs={{0,496},{16,480},{32,464},{48,448},{64,432},{80,416},{96,400},{112... | collective-permute-start | bytes 245768 | tf_op jit(solution)/shard_map/ppermute | solution.py:116
  20.4 14.2 %all_gather.13 = bf16[2,128,1280]{1,2,0:T(8,128)(2,1)S(1)} all-gather(bf16[2,128,160]{1,2,0:T(8,128)(2,1)S(1)} %pad_maximum_fusion.7), channel_id=1, replica_groups=mesh['phase'=32,'tp'=8,'dp'=2] {'tp'}, dimensions={2}, use_global_device_ids=true | all-gather | bytes 737280 | tf_op jit(solution)/shard_map/all_gather | solution.py:86
  40.6 15.4 %all_gather.12 = bf16[2,128,1280]{1,2,0:T(8,128)(2,1)S(1)} all-gather(bf16[2,128,160]{1,2,0:T(8,128)(2,1)S(1)} %pad_maximum_fusion.6), channel_id=1, replica_groups=mesh['phase'=32,'tp'=8,'dp'=2] {'tp'}, dimensions={2}, use_global_device_ids=true | all-gather | bytes 737280 | tf_op jit(solution)/shard_map/all_gather | solution.py:102
  56.0 20.3 %reduce-scatter.4.cloned.1.call-done = bf16[2,128,160]{1,2,0:T(8,128)(2,1)} async-done(((bf16[2,128,1280]{1,2,0:T(8,128)(2,1)}), bf16[2,128,160]{1,2,0:T(8,128)(2,1)}) %reduce-scatter.4.cloned.1.call-update) | async-done | bytes 81936 | tf_op jit(solution)/shard_map/reduce_scatter | solution.py:93
  77.2 3.4 %collective-permute-start.1 = (bf16[2,128,160]{1,2,0:T(8,128)(2,1)S(1)}, bf16[2,128,160]{1,2,0:T(8,128)(2,1)S(1)}, u32[]{:S(2)}, u32[]{:S(2)}) collective-permute-start(bf16[2,128,160]{1,2,0:T(8,128)(2,1)S(1)} %add_convert_fusion.5), channel_id=1, source_target_pairs={{0,16},{16,32},{32,48},{48,64},{64,80},{80,96},{96,112},{112,128},... | collective-permute-start | bytes 245768 | tf_op jit(solution)/shard_map/ppermute | solution.py:14
  80.9 3.2 %collective-permute-done.1 = bf16[2,128,160]{1,2,0:T(8,128)(2,1)S(1)} collective-permute-done((bf16[2,128,160]{1,2,0:T(8,128)(2,1)S(1)}, bf16[2,128,160]{1,2,0:T(8,128)(2,1)S(1)}, u32[]{:S(2)}, u32[]{:S(2)}) %collective-permute-start.1) | collective-permute-done | bytes 81952 | tf_op jit(solution)/shard_map/ppermute | solution.py:14
  84.1 19.2 %all_gather.14 = bf16[2,128,1280]{1,2,0:T(8,128)(2,1)S(1)} all-gather(bf16[2,128,160]{1,2,0:T(8,128)(2,1)S(1)} %collective-permute-done.1), channel_id=1, replica_groups=mesh['phase'=32,'tp'=8,'dp'=2] {'tp'}, dimensions={2}, use_global_device_ids=true | all-gather | bytes 737280 | tf_op jit(solution)/shard_map/all_gather | solution.py:86
  108.9 1.5 convolution_convert_fusion.1
  111.7 2.0 convolution_convert_fusion.3
  113.7 31.1 %reduce-scatter.6.cloned.1.call-done = bf16[2,128,160]{1,2,0:T(8,128)(2,1)} async-done(((bf16[2,128,1280]{1,2,0:T(8,128)(2,1)}), bf16[2,128,160]{1,2,0:T(8,128)(2,1)}) %reduce-scatter.6.cloned.1.call-update) | async-done | bytes 81936 | tf_op jit(solution)/shard_map/reduce_scatter | solution.py:109
  145.7 2.8 collective-permute-start.2
  148.5 2.4 convolution_bitcast_fusion.2
  151.0 3.7 %collective-permute-done.2 = bf16[2,128,160]{1,2,0:T(8,128)(2,1)S(1)} collective-permute-done((bf16[2,128,160]{1,2,0:T(8,128)(2,1)S(1)}, bf16[2,128,160]{1,2,0:T(8,128)(2,1)S(1)}, u32[]{:S(2)}, u32[]{:S(2)}) %collective-permute-start.2) | collective-permute-done | bytes 81952 | tf_op jit(solution)/shard_map/ppermute | solution.py:14
  154.7 19.4 %all_gather.15 = bf16[2,128,1280]{1,2,0:T(8,128)(2,1)S(1)} all-gather(bf16[2,128,160]{1,2,0:T(8,128)(2,1)S(1)} %collective-permute-done.2), channel_id=1, replica_groups=mesh['phase'=32,'tp'=8,'dp'=2] {'tp'}, dimensions={2}, use_global_device_ids=true | all-gather | bytes 737280 | tf_op jit(solution)/shard_map/all_gather | solution.py:102
  177.6 1.5 convolution_convert_fusion
  179.1 2.0 convolution_bitcast_fusion.1
  181.1 1.6 fusion.3
  182.7 2.2 fusion.1
  184.9 1.3 pad_maximum_fusion
  186.2 4.9 %collective-permute-start.4 = (bf16[640,1280]{1,0:T(8,128)(2,1)}, bf16[640,1280]{1,0:T(8,128)(2,1)}, u32[]{:S(2)}, u32[]{:S(2)}) collective-permute-start(bf16[640,1280]{1,0:T(8,128)(2,1)} %pad_maximum_fusion), channel_id=1, source_target_pairs={{0,1},{1,0},{2,3},{3,2},{4,5},{5,4},{6,7},{7,6},{8,9},{9,8},{10,11... | collective-permute-start | bytes 4915208 | tf_op jit(solution)/shard_map/ppermute | solution.py:149
  191.1 81.0 %reduce-scatter.8.cloned.1.call-done = bf16[2,128,160]{1,2,0:T(8,128)(2,1)} async-done(((bf16[2,128,1280]{1,2,0:T(8,128)(2,1)}), bf16[2,128,160]{1,2,0:T(8,128)(2,1)}) %reduce-scatter.8.cloned.1.call-update) | async-done | bytes 81936 | tf_op jit(solution)/shard_map/reduce_scatter | solution.py:109
  273.6 5.3 %collective-permute-start.3 = (bf16[128,160]{0,1:T(8,128)(2,1)S(1)}, bf16[128,160]{0,1:T(8,128)(2,1)S(1)}, u32[]{:S(2)}, u32[]{:S(2)}) collective-permute-start(bf16[128,160]{0,1:T(8,128)(2,1)S(1)} %get-tuple-element.72), channel_id=1, source_target_pairs={{0,496},{16,480},{32,464},{48,448},{64,432},{80,416},{96,400},{112... | collective-permute-start | bytes 122888 | tf_op jit(solution)/shard_map/ppermute | solution.py:116
  279.0 5.7 %collective-permute-done.3 = bf16[128,160]{0,1:T(8,128)(2,1)S(1)} collective-permute-done((bf16[128,160]{0,1:T(8,128)(2,1)S(1)}, bf16[128,160]{0,1:T(8,128)(2,1)S(1)}, u32[]{:S(2)}, u32[]{:S(2)}) %collective-permute-start.3) | collective-permute-done | bytes 40992 | tf_op jit(solution)/shard_map/ppermute | solution.py:116
  284.6 1.8 add_convert_fusion
  (229 shorter events, 29.0 us)
Async XLA Ops:
  7.2 27.5 %copy-start = (bf16[1,3,160,1280]{3,2,1,0:T(8,128)(2,1)S(1)}, bf16[1,3,160,1280]{3,2,1,0:T(8,128)(2,1)}, u32[]{:S(2)}) copy-start(bf16[1,3,160,1280]{3,2,1,0:T(8,128)(2,1)} %param.16) | copy-start | bytes 3686404
  7.2 69.1 %reduce-scatter.4.cloned.1.call-start = ((), (), s32[]{:S(2)}) async-start(), calls=%async_computation.3 | async-start | bytes 737280 | tf_op jit(solution)/shard_map/reduce_scatter | solution.py:93
  8.1 11.5 %collective-permute-start = (bf16[2,128,160]{1,2,0:T(8,128)(2,1)S(1)}, bf16[2,128,160]{1,2,0:T(8,128)(2,1)S(1)}, u32[]{:S(2)}, u32[]{:S(2)}) collective-permute-start(bf16[2,128,160]{1,2,0:T(8,128)(2,1)S(1)} %pad_maximum_fusion.5), channel_id=1, source_target_pairs={{0,496},{16,480},{32,464},{48,448},{64,432},{80,416},{96,400},{112... | collective-permute-start | bytes 245768 | tf_op jit(solution)/shard_map/ppermute | solution.py:116
  19.6 21.0 %copy-start.18 = (bf16[1,128,160]{1,2,0:T(8,128)(2,1)}, bf16[1,128,160]{1,2,0:T(8,128)(2,1)S(1)}, u32[]{:S(2)}) copy-start(bf16[1,128,160]{1,2,0:T(8,128)(2,1)S(1)} %get-tuple-element.74) | copy-start | bytes 122884
  37.8 38.5 %copy-start.20 = (bf16[1,128,160]{1,2,0:T(8,128)(2,1)S(1)}, bf16[1,128,160]{1,2,0:T(8,128)(2,1)}, u32[]{:S(2)}) copy-start(bf16[1,128,160]{1,2,0:T(8,128)(2,1)} %copy-done.19) | copy-start | bytes 122884
  37.8 38.4 %copy-start.28 = (bf16[1,1,128,160]{2,3,1,0:T(8,128)(2,1)S(1)}, bf16[1,1,128,160]{2,3,1,0:T(8,128)(2,1)}, u32[]{:S(2)}) copy-start(bf16[1,1,128,160]{2,3,1,0:T(8,128)(2,1)} %param.9) | copy-start | bytes 122884
  39.1 105.7 %reduce-scatter.6.cloned.1.call-start = ((), (), s32[]{:S(2)}) async-start(), calls=%async_computation.4 | async-start | bytes 737280 | tf_op jit(solution)/shard_map/reduce_scatter | solution.py:109
  56.0 24.9 %copy-start.1 = (bf16[2,128,1280]{1,2,0:T(8,128)(2,1)}, bf16[2,128,1280]{1,2,0:T(8,128)(2,1)S(1)}, u32[]{:S(2)}) copy-start(bf16[2,128,1280]{1,2,0:T(8,128)(2,1)S(1)} %all_gather.12) | copy-start | bytes 1966084
  77.2 6.9 %collective-permute-start.1 = (bf16[2,128,160]{1,2,0:T(8,128)(2,1)S(1)}, bf16[2,128,160]{1,2,0:T(8,128)(2,1)S(1)}, u32[]{:S(2)}, u32[]{:S(2)}) collective-permute-start(bf16[2,128,160]{1,2,0:T(8,128)(2,1)S(1)} %add_convert_fusion.5), channel_id=1, source_target_pairs={{0,16},{16,32},{32,48},{48,64},{64,80},{80,96},{96,112},{112,128},... | collective-permute-start | bytes 245768 | tf_op jit(solution)/shard_map/ppermute | solution.py:14
  110.4 161.7 %reduce-scatter.8.cloned.1.call-start = ((), (), s32[]{:S(2)}) async-start(), calls=%async_computation.5 | async-start | bytes 737280 | tf_op jit(solution)/shard_map/reduce_scatter | solution.py:109
  113.7 60.5 %copy-start.5 = (bf16[1,160,1280]{2,1,0:T(8,128)(2,1)S(1)}, bf16[1,160,1280]{2,1,0:T(8,128)(2,1)}, u32[]{:S(2)}) copy-start(bf16[1,160,1280]{2,1,0:T(8,128)(2,1)} %param.17) | copy-start | bytes 1228804
  145.7 9.0 %collective-permute-start.2 = (bf16[2,128,160]{1,2,0:T(8,128)(2,1)S(1)}, bf16[2,128,160]{1,2,0:T(8,128)(2,1)S(1)}, u32[]{:S(2)}, u32[]{:S(2)}) collective-permute-start(bf16[2,128,160]{1,2,0:T(8,128)(2,1)S(1)} %add_convert_fusion.4), channel_id=1, source_target_pairs={{16,0},{32,16},{48,32},{64,48},{80,64},{96,80},{112,96},{128,112},... | collective-permute-start | bytes 245768 | tf_op jit(solution)/shard_map/ppermute | solution.py:14
  148.5 25.9 %copy-start.26 = (f32[2,2,128,128]{2,3,1,0:T(8,128)S(1)}, f32[2,2,128,128]{2,3,1,0:T(8,128)}, u32[]{:S(2)}) copy-start(f32[2,2,128,128]{2,3,1,0:T(8,128)} %copy-done.25) | copy-start | bytes 786436
  148.5 25.9 %copy-start.31 = (pred[2,128,128]{1,2,0:T(8,128)(4,1)S(1)}, pred[2,128,128]{1,2,0:T(8,128)(4,1)}, u32[]{:S(2)}) copy-start(pred[2,128,128]{1,2,0:T(8,128)(4,1)} %copy-done.30) | copy-start | bytes 98308
  148.5 25.9 %copy-start.57 = (f32[2,2,128]{2,1,0:T(2,128)S(1)}, f32[2,2,128]{2,1,0:T(2,128)}, u32[]{:S(2)}) copy-start(f32[2,2,128]{2,1,0:T(2,128)} %multiply_divide_fusion) | copy-start | bytes 6148
  151.0 24.1 %copy-start.34 = (f32[2,2,128,20]{2,3,1,0:T(8,128)S(1)}, f32[2,2,128,20]{2,3,1,0:T(8,128)}, u32[]{:S(2)}) copy-start(f32[2,2,128,20]{2,3,1,0:T(8,128)} %copy-done.33) | copy-start | bytes 122884
  151.0 24.1 %copy-start.36 = (f32[2,2,128,20]{2,3,1,0:T(8,128)S(1)}, f32[2,2,128,20]{2,3,1,0:T(8,128)}, u32[]{:S(2)}) copy-start(f32[2,2,128,20]{2,3,1,0:T(8,128)} %copy-done.35) | copy-start | bytes 122884
  151.0 24.1 %copy-start.38 = (f32[2,2,128,20]{2,3,1,0:T(8,128)S(1)}, f32[2,2,128,20]{2,3,1,0:T(8,128)}, u32[]{:S(2)}) copy-start(f32[2,2,128,20]{2,3,1,0:T(8,128)} %copy-done.37) | copy-start | bytes 122884
  151.0 24.1 %copy-start.40 = (f32[2,2,128,20]{2,3,1,0:T(8,128)S(1)}, f32[2,2,128,20]{2,3,1,0:T(8,128)}, u32[]{:S(2)}) copy-start(f32[2,2,128,20]{2,3,1,0:T(8,128)} %copy-done.39) | copy-start | bytes 122884
  151.0 24.2 %copy-start.59 = (f32[2,2,128]{2,1,0:T(2,128)S(1)}, f32[2,2,128]{2,1,0:T(2,128)}, u32[]{:S(2)}) copy-start(f32[2,2,128]{2,1,0:T(2,128)} %copy-done.58) | copy-start | bytes 6148
  154.7 21.1 %copy-start.21 = (bf16[2,128,160]{1,2,0:T(8,128)(2,1)}, bf16[2,128,160]{1,2,0:T(8,128)(2,1)S(1)}, u32[]{:S(2)}) copy-start(bf16[2,128,160]{1,2,0:T(8,128)(2,1)S(1)} %collective-permute-done.2) | copy-start | bytes 245764
  184.9 87.2 %copy-start.22 = (bf16[2,128,160]{1,2,0:T(8,128)(2,1)S(1)}, bf16[2,128,160]{1,2,0:T(8,128)(2,1)}, u32[]{:S(2)}) copy-start(bf16[2,128,160]{1,2,0:T(8,128)(2,1)} %copy-done.21) | copy-start | bytes 245764
  186.2 98.4 %collective-permute-start.4 = (bf16[640,1280]{1,0:T(8,128)(2,1)}, bf16[640,1280]{1,0:T(8,128)(2,1)}, u32[]{:S(2)}, u32[]{:S(2)}) collective-permute-start(bf16[640,1280]{1,0:T(8,128)(2,1)} %pad_maximum_fusion), channel_id=1, source_target_pairs={{0,1},{1,0},{2,3},{3,2},{4,5},{5,4},{6,7},{7,6},{8,9},{9,8},{10,11... | collective-permute-start | bytes 4915208 | tf_op jit(solution)/shard_map/ppermute | solution.py:149
  273.6 11.0 %collective-permute-start.3 = (bf16[128,160]{0,1:T(8,128)(2,1)S(1)}, bf16[128,160]{0,1:T(8,128)(2,1)S(1)}, u32[]{:S(2)}, u32[]{:S(2)}) collective-permute-start(bf16[128,160]{0,1:T(8,128)(2,1)S(1)} %get-tuple-element.72), channel_id=1, source_target_pairs={{0,496},{16,480},{32,464},{48,448},{64,432},{80,416},{96,400},{112... | collective-permute-start | bytes 122888 | tf_op jit(solution)/shard_map/ppermute | solution.py:116
  (45 other events, 149.8 us)
Sparse Core Ops, SparseCore 0:
  39.2 36.9 reduce-scatter.3
  110.5 34.2 reduce-scatter.5
  181.2 90.8 reduce-scatter.7

commit v2 on v1

v2 whole, which is shorter than its diff:
```python
import functools
import math

import jax
import jax.numpy as jnp
from jax import lax
from jax.experimental import pallas as pl
from jax.experimental.pallas import tpu as pltpu
from jax.sharding import PartitionSpec as P

HD = 80
QUARTER = 20
TOK = 128
D = 1280
SHARD = 160
CHUNK = 320
CHIPS = 4
HEADS = 4
PHASES = 32
ROWS = 480
MESH = pl.DeviceIdType.MESH
F32 = jnp.float32
BF16 = jnp.bfloat16


def dot_nn(a, b):
    return lax.dot_general(a, b, (((1,), (0,)), ((), ())), preferred_element_type=F32)


def dot_nt(a, b):
    return lax.dot_general(a, b, (((1,), (1,)), ((), ())), preferred_element_type=F32)


def dot_tn(a, b):
    return lax.dot_general(a, b, (((0,), (0,)), ((), ())), preferred_element_type=F32)


def normalize(x):
    centred = x - jnp.mean(x, axis=0, keepdims=True)
    scale = lax.rsqrt(jnp.mean(centred * centred, axis=0, keepdims=True) + 1e-06)
    return centred * scale, scale


def pull_normalize(grad, y, scale):
    return scale * (
        grad
        - jnp.mean(grad, axis=0, keepdims=True)
        - y * jnp.mean(grad * y, axis=0, keepdims=True)
    )


def swap_pairs(y):
    row = lax.broadcasted_iota(jnp.int32, y.shape, 0)
    first = (row < QUARTER) | ((row >= 2 * QUARTER) & (row < 3 * QUARTER))
    return jnp.where(first, pltpu.roll(y, HD - QUARTER, axis=0), pltpu.roll(y, QUARTER, axis=0))


def identity(size):
    row = lax.broadcasted_iota(jnp.int32, (size, size), 0)
    column = lax.broadcasted_iota(jnp.int32, (size, size), 1)
    return jnp.where(row == column, 1.0, 0.0).astype(BF16)


def kernel(
    down_x,
    up_x,
    down_cot,
    up_cot,
    segments,
    patch_rows,
    patch_cols,
    w_qkv,
    w_out,
    out_down,
    out_up,
    out_qkv,
    out_wo,
    staged,
    meta,
    cosine,
    sine,
    mask,
    wq,
    wo,
    wq_t,
    wo_t,
    x1,
    x2,
    g1,
    g2,
    project,
    grad_o,
    ys,
    scales,
    qkv,
    weights,
    heads1,
    heads2,
    dp1,
    dp2,
    partial,
    landed,
    reduced,
    final,
    sums,
    sums_in,
    outgoing,
    load_sem,
    swap_send,
    swap_recv,
    init_send,
    init_recv,
    meta_send,
    meta_recv,
    ag_send,
    ag_recv,
    rs_send,
    rs_recv,
    fin_send,
    fin_recv,
    gw_send,
    gw_recv,
    out_sem,
):
    p = lax.axis_index("phase")
    tp = lax.axis_index("tp")
    d = lax.axis_index("dp")
    c = tp // 2
    k = tp % 2
    mirror = PHASES - 1 - p
    has_next = p < PHASES - 1
    has_last = p > 0
    index1 = jnp.where(k == 0, p, mirror)
    back = jnp.maximum(p - 1, 0)
    index2 = jnp.where(k == 0, back, PHASES - 1 - back)

    def remote(src, dst, send, recv, device):
        return pltpu.make_async_remote_copy(
            src_ref=src,
            dst_ref=dst,
            send_sem=send,
            recv_sem=recv,
            device_id=device,
            device_id_type=MESH,
        )

    def peer(phase, rep, m):
        other = 2 * (c ^ m) + k
        return (phase, other, d if rep == 0 else 1 - d)

    core_mate = (p, 2 * c + 1 - k, d)

    loads = [
        pltpu.make_async_copy(w_qkv, wq.at[0], load_sem.at[0]),
        pltpu.make_async_copy(w_out, wo.at[0], load_sem.at[1]),
    ]
    for copy in loads:
        copy.start()

    barrier = pltpu.get_barrier_semaphore()

    def greet(device):
        pl.semaphore_signal(barrier, inc=1, device_id=device, device_id_type=MESH)

    greet(core_mate)
    for m in range(1, CHIPS):
        greet(peer(p, 0, m))
    for m in range(CHIPS):
        greet(peer(p, 1, m))
    greet((mirror, 2 * c + 1, d))

    @pl.when(k == 1)
    def _():
        greet((mirror, 2 * c, d))

    @pl.when(has_last)
    def _():
        for rep in range(2):
            for m in range(CHIPS):
                greet(peer(p - 1, rep, m))

    @pl.when(has_next)
    def _():
        for rep in range(2):
            for m in range(CHIPS):
                greet(peer(p + 1, rep, m))

    expected = (
        8
        + 1
        + k
        + 8 * jnp.where(has_next, 1, 0)
        + 8 * jnp.where(has_last, 1, 0)
    )

    eye = identity(SHARD)
    for i, ref in enumerate((down_x, up_x, down_cot, up_cot)):
        staged[i] = dot_nt(eye, ref[...]).astype(BF16)
    for tick, index in enumerate((index1, index2)):
        for i, table in enumerate((segments, patch_rows, patch_cols)):
            meta[0, tick, pl.ds(i, 1), :] = table[k, 0, pl.ds(index, 1), :]
        meta[0, tick, 3:8, :] = jnp.zeros((5, TOK), jnp.int32)

    pl.semaphore_wait(barrier, expected)

    def rows_at(start, size):
        return pl.ds(pl.multiple_of(start, SHARD), size)

    full_in = (x1, g2)
    down_init = []
    up_init = []
    for i in range(2):
        spot = full_in[i].at[0, rows_at(c * CHUNK + k * SHARD, SHARD), :]
        up_init.append(
            remote(
                staged.at[2 * i + 1],
                spot,
                init_send.at[i, 0],
                init_recv.at[i, k],
                (mirror, 2 * c + 1, d),
            )
        )
        down_init.append(
            remote(
                staged.at[2 * i],
                spot,
                init_send.at[i, 1],
                init_recv.at[i, k],
                (p, 2 * c, d),
            )
        )
    for i in range(2):
        up_init[i].start()

        @pl.when(k == 1)
        def _():
            down_init[i].start()

        @pl.when(k == 0)
        def _():
            full_in[i][0, rows_at(c * CHUNK, SHARD), :] = staged[2 * i]

    swaps = [
        remote(w_qkv, wq.at[1], swap_send.at[0], swap_recv.at[0], core_mate),
        remote(w_out, wo.at[1], swap_send.at[1], swap_recv.at[1], core_mate),
    ]
    for copy in swaps:
        copy.start()
    meta_copy = remote(meta.at[0], meta.at[1], meta_send, meta_recv, peer(p, 1, 0))
    meta_copy.start()

    def await_init(i):
        def landing(shard):
            spot = full_in[i].at[0, rows_at(c * CHUNK + shard * SHARD, SHARD), :]
            remote(
                staged.at[0], spot, init_send.at[i, 0], init_recv.at[i, shard], core_mate
            ).wait_recv()

        @pl.when(k == 1)
        def _():
            landing(0)

        landing(1)

    def chunk_of(buffer, rep, chip):
        return buffer.at[rep, rows_at(chip * CHUNK, CHUNK), :]

    def gather(n, source, buffer, phase, rep, with_self):
        return [
            remote(
                source,
                chunk_of(buffer, rep, c),
                ag_send.at[n, rep, m],
                ag_recv.at[n, rep, m],
                peer(phase, rep, m),
            )
            for m in (3, 2, 1, 0)
            if m or rep or with_self
        ]

    def await_gather(n, buffer, rep, with_self):
        for m in range(CHIPS):
            if m or rep or with_self:
                remote(
                    reduced.at[0],
                    chunk_of(buffer, rep, c ^ m),
                    ag_send.at[n, rep, m],
                    ag_recv.at[n, rep, m],
                    core_mate,
                ).wait_recv()

    def start(copies):
        for copy in copies:
            copy.start()

    def tables(tick, rep):
        n = 2 * tick + rep
        row = lax.broadcasted_iota(jnp.int32, (HD, TOK), 0)
        power = (row % QUARTER).astype(F32)
        frequency = jnp.exp(power * (-math.log(10000.0) / QUARTER))
        position = jnp.where(
            row < 2 * QUARTER,
            jnp.broadcast_to(meta[rep, tick, 1:2, :], (HD, TOK)),
            jnp.broadcast_to(meta[rep, tick, 2:3, :], (HD, TOK)),
        ).astype(F32)
        angle = position * frequency
        first = (row < QUARTER) | ((row >= 2 * QUARTER) & (row < 3 * QUARTER))
        cosine[n] = jnp.cos(angle)
        turned = jnp.sin(angle)
        sine[n] = jnp.where(first, -turned, turned)
        ids = jnp.broadcast_to(meta[rep, tick, 0:1, :].astype(F32), (TOK, TOK))
        mask[n] = jnp.where(ids == ids.T, 1.0, 0.0)

    def flip_weights(slot):
        small = identity(TOK)

        def body(j, _):
            at = pl.ds(pl.multiple_of(j * TOK, TOK), TOK)
            wq_t[slot, at, :] = dot_nt(small, wq[slot, :, at]).astype(BF16)
            wo_t[slot, at, :] = dot_nt(small, wo[slot, :, at]).astype(BF16)
            return 0

        lax.fori_loop(0, D // TOK, body, 0)

    scale = 1.0 / math.sqrt(HD)

    def forward_head(n, slot, head):
        at = head * HD
        yq, sq = normalize(project[slot, at : at + HD, :])
        yk, sk = normalize(project[slot, SHARD + at : SHARD + at + HD, :])
        v = project[slot, 2 * SHARD + at : 2 * SHARD + at + HD, :].astype(BF16)
        qr = (yq * cosine[n] + swap_pairs(yq) * sine[n]).astype(BF16)
        kr = (yk * cosine[n] + swap_pairs(yk) * sine[n]).astype(BF16)
        raised = jnp.where(mask[n] > 0.5, jnp.exp(dot_tn(kr, qr) * scale), 0.0)
        soft = raised / jnp.sum(raised, axis=0, keepdims=True)
        blended = dot_nn(v, soft.astype(BF16))
        return yq, sq, yk, sk, qr, kr, v, soft, blended.astype(BF16)

    def backward_head(n, state, grad):
        yq, sq, yk, sk, qr, kr, v, soft = state
        gb = grad.astype(BF16)
        d_soft = dot_tn(v, gb)
        mean = jnp.sum(soft * d_soft, axis=0, keepdims=True)
        d_score = (soft * (d_soft - mean)).astype(BF16)
        dv = dot_nt(gb, soft.astype(BF16))
        dq = dot_nn(kr, d_score) * scale
        dk = dot_nt(qr, d_score) * scale
        dq = dq * cosine[n] - swap_pairs(dq) * sine[n]
        dk = dk * cosine[n] - swap_pairs(dk) * sine[n]
        dq = pull_normalize(dq, yq, sq)
        dk = pull_normalize(dk, yk, sk)
        return dq.astype(BF16), dk.astype(BF16), dv.astype(BF16)

    def run_project(buffer, rep):
        x = buffer[rep]
        for slot in range(2):
            project[slot] = dot_nn(wq[slot], x)

    def run_grad_o(buffer, rep):
        g = buffer[rep]
        for slot in range(2):
            grad_o[slot] = dot_nn(wo[slot], g)

    def forward_first(rep):
        run_project(x1, rep)

        def body(slot, _):
            for head in range(2):
                yq, sq, yk, sk, qr, kr, v, soft, o = forward_head(rep, slot, head)
                ys[rep, slot, head, 0] = yq
                ys[rep, slot, head, 1] = yk
                scales[rep, slot, head, 0:1, :] = sq
                scales[rep, slot, head, 1:2, :] = sk
                qkv[rep, slot, head, 0] = qr
                qkv[rep, slot, head, 1] = kr
                qkv[rep, slot, head, 2] = v
                weights[rep, slot, head] = soft
                heads1[rep, slot, head * HD : (head + 1) * HD, :] = o
            return 0

        lax.fori_loop(0, 2, body, 0)

    def keep(buffer, rep, slot, head, grads):
        for i in range(3):
            at = i * SHARD + head * HD
            buffer[rep, slot, at : at + HD, :] = grads[i]

    def both_second(rep):
        run_project(x2, rep)

        def body(slot, _):
            for head in range(2):
                values = forward_head(2 + rep, slot, head)
                heads2[rep, slot, head * HD : (head + 1) * HD, :] = values[8]
                grad = grad_o[slot, head * HD : (head + 1) * HD, :]
                keep(dp2, rep, slot, head, backward_head(2 + rep, values[:8], grad))
            return 0

        lax.fori_loop(0, 2, body, 0)

    def backward_first(rep):
        def body(slot, _):
            for head in range(2):
                state = (
                    ys[rep, slot, head, 0],
                    scales[rep, slot, head, 0:1, :],
                    ys[rep, slot, head, 1],
                    scales[rep, slot, head, 1:2, :],
                    qkv[rep, slot, head, 0],
                    qkv[rep, slot, head, 1],
                    qkv[rep, slot, head, 2],
                    weights[rep, slot, head],
                )
                grad = grad_o[slot, head * HD : (head + 1) * HD, :]
                keep(dp1, rep, slot, head, backward_head(rep, state, grad))
            return 0

        lax.fori_loop(0, 2, body, 0)

    def send_partials(n, flipped, small):
        copies = []
        for m in (3, 2, 1, 0):
            at = rows_at((c ^ m) * CHUNK, CHUNK)
            total = dot_nn(flipped[0, at, :], small[0, 0]) + dot_nn(
                flipped[1, at, :], small[0, 1]
            )
            if m == 0:
                partial[n, 0] = total
            else:
                outgoing[n, m - 1] = total.astype(BF16)
                copies.append(
                    remote(
                        outgoing.at[n, m - 1],
                        landed.at[n, m - 1],
                        rs_send.at[n, m - 1],
                        rs_recv.at[n, m - 1],
                        peer(p, 0, m),
                    )
                )
                copies[-1].start()
        return copies

    def reduce_partials(n, copies, residual):
        total = residual[0, rows_at(c * CHUNK, CHUNK), :].astype(F32) + partial[n, 0]
        for copy in copies:
            copy.wait_recv()
        for m in range(1, CHIPS):
            total = total + landed[n, m - 1].astype(F32)
        reduced[n] = total.astype(BF16)

    await_init(0)
    chunk = chunk_of(x1, 0, c)
    x1_own = gather(0, chunk, x1, p, 0, False)
    start(x1_own)
    tables(0, 0)
    for copy in loads:
        copy.wait()
    flip_weights(0)
    await_init(1)
    cot_chunk = chunk_of(g2, 0, c)
    cot_own = gather(1, cot_chunk, g2, p, 0, False)
    start(cot_own)
    for copy in swaps:
        copy.wait_recv()
    flip_weights(1)
    await_gather(0, x1, 0, False)
    forward_first(0)
    rs1 = send_partials(0, wo_t, heads1)
    x1_other = gather(0, chunk, x1, p, 1, False)
    start(x1_other)
    meta_copy.wait_recv()
    tables(1, 0)
    tables(0, 1)
    tables(1, 1)
    reduce_partials(0, rs1, x1)

    x2_own = gather(2, reduced.at[0], x2, p + 1, 0, True)
    x2_other = gather(2, reduced.at[0], x2, p + 1, 1, True)

    @pl.when(has_next)
    def _():
        start(x2_own)

    cot_other = gather(1, cot_chunk, g2, p, 1, False)
    start(cot_other)

    @pl.when(has_next)
    def _():
        start(x2_other)

    await_gather(0, x1, 1, False)
    forward_first(1)
    await_gather(1, g2, 0, False)
    run_grad_o(g2, 0)

    @pl.when(has_last)
    def _():
        await_gather(2, x2, 0, True)

    @pl.when(p == 0)
    def _():
        x2[...] = jnp.zeros_like(x2)

    both_second(0)
    rs2 = send_partials(1, wq_t, dp2)

    await_gather(1, g2, 1, False)
    run_grad_o(g2, 1)

    @pl.when(has_last)
    def _():
        await_gather(2, x2, 1, True)

    both_second(1)
    reduce_partials(1, rs2, g2)
    g1_own = gather(3, reduced.at[1], g1, p - 1, 0, True)
    g1_other = gather(3, reduced.at[1], g1, p - 1, 1, True)

    @pl.when(has_last)
    def _():
        start(g1_own)
        start(g1_other)

    def gradient(slot, j, tick):
        dps, xs = (dp1, x1) if tick == 0 else (dp2, x2)
        at = pl.ds(pl.multiple_of(j * SHARD, SHARD), SHARD)
        left = jnp.concatenate([dps[0, slot, at, :], dps[1, slot, at, :]], axis=1)
        right = jnp.concatenate([xs[0], xs[1]], axis=1)
        return dot_nt(left, right)

    def gradient_out(slot, tick):
        hs, gs = (heads1, g1) if tick == 0 else (heads2, g2)
        left = jnp.concatenate([hs[0, slot], hs[1, slot]], axis=1)
        right = jnp.concatenate([gs[0], gs[1]], axis=1)
        return dot_nt(left, right)

    def second_sums(i, _):
        slot = i // 3
        j = i % 3
        sums[slot, j] = gradient(slot, j, 1)
        return 0

    lax.fori_loop(0, 6, second_sums, 0)
    for slot in range(2):
        sums[slot, 3] = gradient_out(slot, 1)

    @pl.when(has_next)
    def _():
        await_gather(3, g1, 0, True)

    @pl.when(p == PHASES - 1)
    def _():
        g1[...] = jnp.zeros_like(g1)

    run_grad_o(g1, 0)
    backward_first(0)
    rs3 = send_partials(2, wq_t, dp1)

    @pl.when(has_next)
    def _():
        await_gather(3, g1, 1, True)

    run_grad_o(g1, 1)
    backward_first(1)
    reduce_partials(2, rs3, g1)

    up_fin = [
        remote(
            reduced.at[2, pl.ds(s * SHARD, SHARD), :],
            final.at[1],
            fin_send.at[s],
            fin_recv.at[1],
            (mirror, 2 * c + s, d),
        )
        for s in range(2)
    ]
    down_fin = remote(
        reduced.at[2, pl.ds(SHARD, SHARD), :], final.at[0], fin_send.at[0], fin_recv.at[0], core_mate
    )

    @pl.when(k == 1)
    def _():
        start(up_fin)

    @pl.when(k == 0)
    def _():
        down_fin.start()
        final[0] = reduced[2, 0:SHARD, :]

    handed = [
        remote(sums_in.at[0, j], sums_in.at[1, j], gw_send.at[j], gw_recv.at[j], core_mate)
        for j in range(4)
    ]
    for j in range(4):
        more = gradient(1, j, 0) if j < 3 else gradient_out(1, 0)
        sums_in[0, j] = (sums[1, j] + more).astype(BF16)
        handed[j].start()
    results = []
    for j in range(4):
        more = gradient(0, j, 0) if j < 3 else gradient_out(0, 0)
        total = sums[0, j] + more
        handed[j].wait_recv()
        sums_in[2, j] = (total + sums_in[1, j].astype(F32)).astype(BF16)
        target = out_qkv.at[pl.ds(j * SHARD, SHARD), :] if j < 3 else out_wo
        results.append(pltpu.make_async_copy(sums_in.at[2, j], target, out_sem.at[j]))
        results[-1].start()

    @pl.when(k == 1)
    def _():
        remote(staged.at[0], final.at[0], fin_send.at[0], fin_recv.at[0], core_mate).wait_recv()

    remote(staged.at[0], final.at[1], fin_send.at[0], fin_recv.at[1], core_mate).wait_recv()
    small = identity(TOK)
    out_down[...] = dot_nt(small, final[0]).astype(BF16)
    out_up[...] = dot_nt(small, final[1]).astype(BF16)

    for copy in up_init + swaps + [meta_copy] + x1_own + x1_other + cot_own + cot_other:
        copy.wait_send()
    for copy in rs1 + rs2 + rs3 + handed:
        copy.wait_send()

    @pl.when(k == 1)
    def _():
        for copy in down_init + up_fin:
            copy.wait_send()

    @pl.when(k == 0)
    def _():
        down_fin.wait_send()

    @pl.when(has_next)
    def _():
        for copy in x2_own + x2_other:
            copy.wait_send()

    @pl.when(has_last)
    def _():
        for copy in g1_own + g1_other:
            copy.wait_send()

    for copy in results:
        copy.wait()


def per_device(
    down_inputs, up_inputs, down_cot, up_cot, segment_ids, patch_rows, patch_cols, w_qkv, w_out
):
    vmem = pl.BlockSpec(memory_space=pltpu.VMEM)
    hbm = pl.BlockSpec(memory_space=pl.ANY)
    dma = pltpu.SemaphoreType.DMA
    tok_block = jax.ShapeDtypeStruct((TOK, SHARD), BF16)
    outs = pl.pallas_call(
        kernel,
        out_shape=(
            tok_block,
            tok_block,
            jax.ShapeDtypeStruct((ROWS, D), BF16),
            jax.ShapeDtypeStruct((SHARD, D), BF16),
        ),
        in_specs=[vmem] * 7 + [hbm] * 2,
        out_specs=(vmem, vmem, hbm, hbm),
        scratch_shapes=[
            pltpu.VMEM((4, SHARD, TOK), BF16),
            pltpu.VMEM((2, 2, 8, TOK), jnp.int32),
            pltpu.VMEM((4, HD, TOK), F32),
            pltpu.VMEM((4, HD, TOK), F32),
            pltpu.VMEM((4, TOK, TOK), F32),
            pltpu.VMEM((2, ROWS, D), BF16),
            pltpu.VMEM((2, SHARD, D), BF16),
            pltpu.VMEM((2, D, ROWS), BF16),
            pltpu.VMEM((2, D, SHARD), BF16),
            pltpu.VMEM((2, D, TOK), BF16),
            pltpu.VMEM((2, D, TOK), BF16),
            pltpu.VMEM((2, D, TOK), BF16),
            pltpu.VMEM((2, D, TOK), BF16),
            pltpu.VMEM((2, ROWS, TOK), F32),
            pltpu.VMEM((2, SHARD, TOK), F32),
            pltpu.VMEM((2, 2, 2, 2, HD, TOK), F32),
            pltpu.VMEM((2, 2, 2, 8, TOK), F32),
            pltpu.VMEM((2, 2, 2, 3, HD, TOK), BF16),
            pltpu.VMEM((2, 2, 2, TOK, TOK), F32),
            pltpu.VMEM((2, 2, SHARD, TOK), BF16),
            pltpu.VMEM((2, 2, SHARD, TOK), BF16),
            pltpu.VMEM((2, 2, ROWS, TOK), BF16),
            pltpu.VMEM((2, 2, ROWS, TOK), BF16),
            pltpu.VMEM((3, 1, CHUNK, TOK), F32),
            pltpu.VMEM((3, 3, CHUNK, TOK), BF16),
            pltpu.VMEM((3, CHUNK, TOK), BF16),
            pltpu.VMEM((2, SHARD, TOK), BF16),
            pltpu.VMEM((2, 4, SHARD, D), F32),
            pltpu.VMEM((3, 4, SHARD, D), BF16),
            pltpu.VMEM((3, 3, CHUNK, TOK), BF16),
            dma((2,)),
            dma((2,)),
            dma((2,)),
            dma((2, 2)),
            dma((2, 2)),
            dma,
            dma,
            dma((4, 2, 4)),
            dma((4, 2, 4)),
            dma((3, 3)),
            dma((3, 3)),
            dma((2,)),
            dma((2,)),
            dma((4,)),
            dma((4,)),
            dma((4,)),
        ],
        compiler_params=pltpu.CompilerParams(
            collective_id=0, has_side_effects=True, vmem_limit_bytes=48 << 20
        ),
    )(
        down_inputs[0, 0],
        up_inputs[0, 0],
        down_cot[0, 0],
        up_cot[0, 0],
        segment_ids,
        patch_rows,
        patch_cols,
        w_qkv.reshape(ROWS, D),
        w_out[0],
    )
    return (
        outs[0][None, None],
        outs[1][None, None],
        outs[2].reshape(w_qkv.shape),
        outs[3][None],
    )


def solution(mesh):
    return jax.shard_map(
        per_device,
        mesh=mesh,
        in_specs=(
            P("dp", "phase", None, "tp"),
            P("dp", "phase", None, "tp"),
            P("dp", "phase", None, "tp"),
            P("dp", "phase", None, "tp"),
            P(None, "dp", None, None),
            P(None, "dp", None, None),
            P(None, "dp", None, None),
            P("phase", None, "tp", None),
            P("phase", "tp", None),
        ),
        out_specs=(
            P("dp", "phase", None, "tp"),
            P("dp", "phase", None, "tp"),
            P("phase", None, "tp", None),
            P("phase", "tp", None),
        ),
        check_vma=False,
    )
```

time: 296 us -> 128 us (0.43)
  the two profiles are of different devices: /device:TPU:150 before, /device:TPU:3 now
where the time goes in v2:
time: 128 us; the launch traced here: 127 us
  Pallas kernels  115 us (90%)
  local copies, waits for them, and re-layouts  11.3 us (9%)
    pallas_call x1, Pallas kernels, per_device(): pl.pallas_call(kernel, out_shape=(tok_block, tok_block, jax.ShapeDtypeStr...  115 us
    unnamed x18, local copies, waits for them, and re-layouts  11.3 us

profile of v2, /device:TPU:3, one launch (start us, length us, event | category | flops | bytes accessed | tf_op | source)
XLA Modules:
  0.0 127.1 jit_solution(1053512868197542499)
XLA Ops:
  0.6 0.9 copy.13
  1.5 0.9 copy.14
  2.4 0.9 copy.15
  3.3 0.9 copy.16
  4.2 0.0 copy-start
  4.2 1.3 %copy-done = bf16[1,3,160,1280]{3,2,1,0:T(8,128)(2,1)S(1)} copy-done((bf16[1,3,160,1280]{3,2,1,0:T(8,128)(2,1)S(1)}, bf16[1,3,160,1280]{3,2,1,0:T(8,128)(2,1)}, u32[]{:S(2)}) %copy-start) | copy-done | bytes 1228824
  5.5 0.0 copy-start.1
  5.5 1.0 copy-done.1
  6.5 0.0 copy-start.2
  6.5 0.8 copy-done.2
  7.2 0.0 copy-start.3
  7.2 0.8 copy-done.3
  8.0 0.0 copy-start.4
  8.0 0.8 copy-done.4
  8.7 115.1 %shard_map.120 = (bf16[128,160]{1,0:T(8,128)(2,1)S(1)}, bf16[128,160]{1,0:T(8,128)(2,1)S(1)}, bf16[480,1280]{1,0:T(8,128)(2,1)S(1)}, bf16[160,1280]{1,0:T(8,128)(2,1)S(1)}) custom-call(bf16[128,160]{1,0:T(8,128)(2,1)S(1)} %bitcast.14, bf16[128,160]{1,0:T(8,128)(2,1)S(1)} %bitcast.15, bf16[128,160]{1,0:T(8,128)(2,1)S(1)} %bitcast.16, ...), custom_call_target="tpu_custom_call" | custom-call | tf_op jit(solution)/shard_map/pallas_call | solution.py:652
  123.8 0.7 copy.17
  124.6 0.7 copy.18
  125.3 1.0 copy.21
  126.3 0.8 copy.22
Async XLA Ops:
  4.2 1.3 %copy-start = (bf16[1,3,160,1280]{3,2,1,0:T(8,128)(2,1)S(1)}, bf16[1,3,160,1280]{3,2,1,0:T(8,128)(2,1)}, u32[]{:S(2)}) copy-start(bf16[1,3,160,1280]{3,2,1,0:T(8,128)(2,1)} %param.16) | copy-start | bytes 3686404
  5.5 1.0 copy-start.1
  6.5 0.8 copy-start.2
  7.2 0.8 copy-start.3
  8.0 0.8 copy-start.4

commit v3 on v2

--- a/solution.py
+++ b/solution.py
@@ -75,7 +75,7 @@
     out_up,
     out_qkv,
     out_wo,
-    staged,
+    tables_in,
     meta,
     cosine,
     sine,
@@ -114,6 +114,8 @@
     meta_recv,
     ag_send,
     ag_recv,
+    relay_send,
+    relay_recv,
     rs_send,
     rs_recv,
     fin_send,
@@ -150,6 +152,10 @@
 
     core_mate = (p, 2 * c + 1 - k, d)
 
+    def start(copies):
+        for copy in copies:
+            copy.start()
+
     loads = [
         pltpu.make_async_copy(w_qkv, wq.at[0], load_sem.at[0]),
         pltpu.make_async_copy(w_out, wo.at[0], load_sem.at[1]),
@@ -175,9 +181,8 @@
 
     @pl.when(has_last)
     def _():
-        for rep in range(2):
-            for m in range(CHIPS):
-                greet(peer(p - 1, rep, m))
+        for m in range(CHIPS):
+            greet(peer(p - 1, 0, m))
 
     @pl.when(has_next)
     def _():
@@ -189,17 +194,16 @@
         8
         + 1
         + k
-        + 8 * jnp.where(has_next, 1, 0)
+        + 4 * jnp.where(has_next, 1, 0)
         + 8 * jnp.where(has_last, 1, 0)
     )
 
-    eye = identity(SHARD)
-    for i, ref in enumerate((down_x, up_x, down_cot, up_cot)):
-        staged[i] = dot_nt(eye, ref[...]).astype(BF16)
-    for tick, index in enumerate((index1, index2)):
-        for i, table in enumerate((segments, patch_rows, patch_cols)):
-            meta[0, tick, pl.ds(i, 1), :] = table[k, 0, pl.ds(index, 1), :]
-        meta[0, tick, 3:8, :] = jnp.zeros((5, TOK), jnp.int32)
+    table_loads = [
+        pltpu.make_async_copy(table.at[k, 0], tables_in.at[i], load_sem.at[2 + i])
+        for i, table in enumerate((segments, patch_rows, patch_cols))
+    ]
+    for copy in table_loads:
+        copy.start()
 
     pl.semaphore_wait(barrier, expected)
 
@@ -207,13 +211,16 @@
         return pl.ds(pl.multiple_of(start, SHARD), size)
 
     full_in = (x1, g2)
+    downs = (down_x, down_cot)
+    ups = (up_x, up_cot)
     down_init = []
     up_init = []
+    down_local = []
     for i in range(2):
         spot = full_in[i].at[0, rows_at(c * CHUNK + k * SHARD, SHARD), :]
         up_init.append(
             remote(
-                staged.at[2 * i + 1],
+                ups[i],
                 spot,
                 init_send.at[i, 0],
                 init_recv.at[i, k],
@@ -222,13 +229,18 @@
         )
         down_init.append(
             remote(
-                staged.at[2 * i],
+                downs[i],
                 spot,
                 init_send.at[i, 1],
                 init_recv.at[i, k],
                 (p, 2 * c, d),
             )
         )
+        down_local.append(
+            pltpu.make_async_copy(
+                downs[i], full_in[i].at[0, rows_at(c * CHUNK, SHARD), :], load_sem.at[5 + i]
+            )
+        )
     for i in range(2):
         up_init[i].start()
 
@@ -238,14 +250,22 @@
 
         @pl.when(k == 0)
         def _():
-            full_in[i][0, rows_at(c * CHUNK, SHARD), :] = staged[2 * i]
+            down_local[i].start()
 
     swaps = [
         remote(w_qkv, wq.at[1], swap_send.at[0], swap_recv.at[0], core_mate),
         remote(w_out, wo.at[1], swap_send.at[1], swap_recv.at[1], core_mate),
     ]
-    for copy in swaps:
-        copy.start()
+    @pl.when(k == 1)
+    def _():
+        start(swaps)
+
+    for copy in table_loads:
+        copy.wait()
+    for tick, index in enumerate((index1, index2)):
+        for i in range(3):
+            meta[0, tick, pl.ds(i, 1), :] = tables_in[i, pl.ds(index, 1), :]
+        meta[0, tick, 3:8, :] = jnp.zeros((5, TOK), jnp.int32)
     meta_copy = remote(meta.at[0], meta.at[1], meta_send, meta_recv, peer(p, 1, 0))
     meta_copy.start()
 
@@ -253,12 +273,16 @@
         def landing(shard):
             spot = full_in[i].at[0, rows_at(c * CHUNK + shard * SHARD, SHARD), :]
             remote(
-                staged.at[0], spot, init_send.at[i, 0], init_recv.at[i, shard], core_mate
+                downs[0], spot, init_send.at[i, 0], init_recv.at[i, shard], core_mate
             ).wait_recv()
 
         @pl.when(k == 1)
         def _():
             landing(0)
+
+        @pl.when(k == 0)
+        def _():
+            down_local[i].wait()
 
         landing(1)
 
@@ -288,10 +312,6 @@
                     ag_recv.at[n, rep, m],
                     core_mate,
                 ).wait_recv()
-
-    def start(copies):
-        for copy in copies:
-            copy.start()
 
     def tables(tick, rep):
         n = 2 * tick + rep
@@ -448,50 +468,146 @@
             total = total + landed[n, m - 1].astype(F32)
         reduced[n] = total.astype(BF16)
 
+    half = 2 * CHUNK
+
+    def relay(n, buffer):
+        def piece(rep, start):
+            return buffer.at[rep, pl.ds(start, half), :]
+
+        def hand(start, chip, s):
+            return remote(
+                piece(0, start),
+                piece(1, start),
+                relay_send.at[n, s],
+                relay_recv.at[n, 0],
+                (p, 2 * chip + k, 1 - d),
+            )
+
+        first = [hand(0, 3, 0), hand(0, 1, 1)]
+        last = [hand(half, 0, 0), hand(half, 2, 1)]
+        mine = pl.multiple_of((1 - c % 2) * half, half)
+        other = pl.multiple_of((c % 2) * half, half)
+        onward = remote(
+            piece(1, mine), piece(1, mine), relay_send.at[n, 2], relay_recv.at[n, 1], peer(p, 0, 1)
+        )
+
+        def begin():
+            @pl.when(c == 0)
+            def _():
+                start(first)
+
+            @pl.when(c == 3)
+            def _():
+                start(last)
+
+        def forward():
+            remote(
+                piece(0, 0), piece(1, mine), relay_send.at[n, 0], relay_recv.at[n, 0], core_mate
+            ).wait_recv()
+            onward.start()
+
+        def finish():
+            remote(
+                piece(0, 0), piece(1, other), relay_send.at[n, 0], relay_recv.at[n, 1], core_mate
+            ).wait_recv()
+
+        def drain():
+            onward.wait_send()
+
+            @pl.when(c == 0)
+            def _():
+                for copy in first:
+                    copy.wait_send()
+
+            @pl.when(c == 3)
+            def _():
+                for copy in last:
+                    copy.wait_send()
+
+        return begin, forward, finish, drain
+
+    def direct(n, source, buffer, phase):
+        chip = jnp.where(c >= 2, 0, 1)
+        return [
+            remote(
+                source,
+                chunk_of(buffer, 1, c),
+                ag_send.at[n, 1, i],
+                ag_recv.at[n, 1, c % 2],
+                (phase, 2 * (chip + 2 * i) + k, 1 - d),
+            )
+            for i in range(2)
+        ]
+
+    def direct_relay(n, buffer):
+        mine = pl.multiple_of((1 - c % 2) * half, half)
+        other = pl.multiple_of((c % 2) * half, half)
+
+        def piece(start):
+            return buffer.at[1, pl.ds(start, half), :]
+
+        onward = remote(
+            piece(mine), piece(mine), relay_send.at[3, 2], relay_recv.at[3, 1], peer(p, 0, 1)
+        )
+
+        def forward():
+            for i in range(2):
+                remote(
+                    reduced.at[0],
+                    buffer.at[1, pl.ds(pl.multiple_of(mine + i * CHUNK, CHUNK), CHUNK), :],
+                    ag_send.at[n, 1, i],
+                    ag_recv.at[n, 1, i],
+                    core_mate,
+                ).wait_recv()
+            onward.start()
+
+        def finish():
+            remote(
+                piece(mine), piece(other), relay_send.at[3, 2], relay_recv.at[3, 1], core_mate
+            ).wait_recv()
+
+        return forward, finish, onward
+
+    x1_relay = relay(0, x1)
+    x2_relay = relay(1, x2)
+    cot_relay = relay(2, g2)
+
     await_init(0)
-    chunk = chunk_of(x1, 0, c)
-    x1_own = gather(0, chunk, x1, p, 0, False)
+    x1_own = gather(0, chunk_of(x1, 0, c), x1, p, 0, False)
     start(x1_own)
+
+    @pl.when(k == 0)
+    def _():
+        start(swaps)
+
     tables(0, 0)
     for copy in loads:
         copy.wait()
     flip_weights(0)
     await_init(1)
-    cot_chunk = chunk_of(g2, 0, c)
-    cot_own = gather(1, cot_chunk, g2, p, 0, False)
-    start(cot_own)
+    cot_own = gather(1, chunk_of(g2, 0, c), g2, p, 0, False)
     for copy in swaps:
         copy.wait_recv()
     flip_weights(1)
     await_gather(0, x1, 0, False)
+    start(cot_own)
     forward_first(0)
     rs1 = send_partials(0, wo_t, heads1)
-    x1_other = gather(0, chunk, x1, p, 1, False)
-    start(x1_other)
+    tables(1, 0)
     meta_copy.wait_recv()
-    tables(1, 0)
     tables(0, 1)
     tables(1, 1)
     reduce_partials(0, rs1, x1)
 
     x2_own = gather(2, reduced.at[0], x2, p + 1, 0, True)
-    x2_other = gather(2, reduced.at[0], x2, p + 1, 1, True)
 
     @pl.when(has_next)
     def _():
         start(x2_own)
 
-    cot_other = gather(1, cot_chunk, g2, p, 1, False)
-    start(cot_other)
-
-    @pl.when(has_next)
-    def _():
-        start(x2_other)
-
-    await_gather(0, x1, 1, False)
-    forward_first(1)
     await_gather(1, g2, 0, False)
     run_grad_o(g2, 0)
+    x1_relay[0]()
 
     @pl.when(has_last)
     def _():
@@ -499,27 +615,26 @@
 
     @pl.when(p == 0)
     def _():
-        x2[...] = jnp.zeros_like(x2)
-
+        x2[0] = jnp.zeros_like(x2[0])
+
+    x2_relay[0]()
+    cot_relay[0]()
     both_second(0)
     rs2 = send_partials(1, wq_t, dp2)
-
-    await_gather(1, g2, 1, False)
-    run_grad_o(g2, 1)
-
-    @pl.when(has_last)
-    def _():
-        await_gather(2, x2, 1, True)
-
-    both_second(1)
+    x1_relay[1]()
     reduce_partials(1, rs2, g2)
     g1_own = gather(3, reduced.at[1], g1, p - 1, 0, True)
-    g1_other = gather(3, reduced.at[1], g1, p - 1, 1, True)
+    g1_other = direct(3, reduced.at[1], g1, p - 1)
+    g1_forward, g1_finish, g1_onward = direct_relay(3, g1)
 
     @pl.when(has_last)
     def _():
         start(g1_own)
         start(g1_other)
+
+    x2_relay[1]()
+    x1_relay[2]()
+    forward_first(1)
 
     def gradient(slot, j, tick):
         dps, xs = (dp1, x1) if tick == 0 else (dp2, x2)
@@ -540,28 +655,30 @@
         sums[slot, j] = gradient(slot, j, 1)
         return 0
 
+    @pl.when(has_next)
+    def _():
+        await_gather(3, g1, 0, True)
+
+    @pl.when(p == PHASES - 1)
+    def _():
+        g1[...] = jnp.zeros_like(g1)
+
+    cot_relay[1]()
+    run_grad_o(g1, 0)
+    backward_first(0)
+    rs3 = send_partials(2, wq_t, dp1)
+
+    @pl.when(has_next)
+    def _():
+        g1_forward()
+
+    cot_relay[2]()
+    run_grad_o(g2, 1)
+    x2_relay[2]()
+    both_second(1)
     lax.fori_loop(0, 6, second_sums, 0)
     for slot in range(2):
         sums[slot, 3] = gradient_out(slot, 1)
-
-    @pl.when(has_next)
-    def _():
-        await_gather(3, g1, 0, True)
-
-    @pl.when(p == PHASES - 1)
-    def _():
-        g1[...] = jnp.zeros_like(g1)
-
-    run_grad_o(g1, 0)
-    backward_first(0)
-    rs3 = send_partials(2, wq_t, dp1)
-
-    @pl.when(has_next)
-    def _():
-        await_gather(3, g1, 1, True)
-
-    run_grad_o(g1, 1)
-    backward_first(1)
     reduce_partials(2, rs3, g1)
 
     up_fin = [
@@ -578,6 +695,10 @@
         reduced.at[2, pl.ds(SHARD, SHARD), :], final.at[0], fin_send.at[0], fin_recv.at[0], core_mate
     )
 
+    down_kept = pltpu.make_async_copy(
+        reduced.at[2, pl.ds(0, SHARD), :], final.at[0], load_sem.at[7]
+    )
+
     @pl.when(k == 1)
     def _():
         start(up_fin)
@@ -585,7 +706,14 @@
     @pl.when(k == 0)
     def _():
         down_fin.start()
-        final[0] = reduced[2, 0:SHARD, :]
+        down_kept.start()
+
+    @pl.when(has_next)
+    def _():
+        g1_finish()
+
+    run_grad_o(g1, 1)
+    backward_first(1)
 
     handed = [
         remote(sums_in.at[0, j], sums_in.at[1, j], gw_send.at[j], gw_recv.at[j], core_mate)
@@ -607,15 +735,21 @@
 
     @pl.when(k == 1)
     def _():
-        remote(staged.at[0], final.at[0], fin_send.at[0], fin_recv.at[0], core_mate).wait_recv()
-
-    remote(staged.at[0], final.at[1], fin_send.at[0], fin_recv.at[1], core_mate).wait_recv()
-    small = identity(TOK)
-    out_down[...] = dot_nt(small, final[0]).astype(BF16)
-    out_up[...] = dot_nt(small, final[1]).astype(BF16)
-
-    for copy in up_init + swaps + [meta_copy] + x1_own + x1_other + cot_own + cot_other:
+        remote(downs[0], final.at[0], fin_send.at[0], fin_recv.at[0], core_mate).wait_recv()
+
+    @pl.when(k == 0)
+    def _():
+        down_kept.wait()
+
+    remote(downs[0], final.at[1], fin_send.at[0], fin_recv.at[1], core_mate).wait_recv()
+    for i, target in enumerate((out_down, out_up)):
+        results.append(pltpu.make_async_copy(final.at[i], target, out_sem.at[4 + i]))
+        results[-1].start()
+
+    for copy in up_init + swaps + [meta_copy] + x1_own + cot_own:
         copy.wait_send()
+    for line in (x1_relay, x2_relay, cot_relay):
+        line[3]()
     for copy in rs1 + rs2 + rs3 + handed:
         copy.wait_send()
 
@@ -630,7 +764,7 @@
 
     @pl.when(has_next)
     def _():
-        for copy in x2_own + x2_other:
+        for copy in x2_own:
             copy.wait_send()
 
     @pl.when(has_last)
@@ -638,29 +772,56 @@
         for copy in g1_own + g1_other:
             copy.wait_send()
 
+    @pl.when(has_next)
+    def _():
+        g1_onward.wait_send()
+
     for copy in results:
+        copy.wait()
+
+
+def place(*refs):
+    sources, targets, kept, sem = refs[:4], refs[4:8], refs[8:12], refs[12]
+    pieces = []
+    for i, count in enumerate((1, 1, 6, 2)):
+        rows = sources[i].shape[0] // count
+        pieces += [(i, pl.ds(j * rows, rows)) for j in range(count)]
+    inward = [
+        pltpu.make_async_copy(sources[i].at[at], kept[i].at[at], sem.at[0, n])
+        for n, (i, at) in enumerate(pieces)
+    ]
+    outward = [
+        pltpu.make_async_copy(kept[i].at[at], targets[i].at[at], sem.at[1, n])
+        for n, (i, at) in enumerate(pieces)
+    ]
+    for copy in inward:
+        copy.start()
+    for before, copy in zip(inward, outward):
+        before.wait()
+        copy.start()
+    for copy in outward:
         copy.wait()
 
 
 def per_device(
     down_inputs, up_inputs, down_cot, up_cot, segment_ids, patch_rows, patch_cols, w_qkv, w_out
 ):
-    vmem = pl.BlockSpec(memory_space=pltpu.VMEM)
-    hbm = pl.BlockSpec(memory_space=pl.ANY)
+    hbm = pl.BlockSpec(memory_space=pltpu.HBM)
     dma = pltpu.SemaphoreType.DMA
-    tok_block = jax.ShapeDtypeStruct((TOK, SHARD), BF16)
+    tok_block = jax.ShapeDtypeStruct((SHARD, TOK), BF16)
+    shapes = (
+        tok_block,
+        tok_block,
+        jax.ShapeDtypeStruct((ROWS, D), BF16),
+        jax.ShapeDtypeStruct((SHARD, D), BF16),
+    )
     outs = pl.pallas_call(
         kernel,
-        out_shape=(
-            tok_block,
-            tok_block,
-            jax.ShapeDtypeStruct((ROWS, D), BF16),
-            jax.ShapeDtypeStruct((SHARD, D), BF16),
-        ),
-        in_specs=[vmem] * 7 + [hbm] * 2,
-        out_specs=(vmem, vmem, hbm, hbm),
+        out_shape=shapes,
+        in_specs=[hbm] * 9,
+        out_specs=(hbm,) * 4,
         scratch_shapes=[
-            pltpu.VMEM((4, SHARD, TOK), BF16),
+            pltpu.VMEM((3, PHASES, TOK), jnp.int32),
             pltpu.VMEM((2, 2, 8, TOK), jnp.int32),
             pltpu.VMEM((4, HD, TOK), F32),
             pltpu.VMEM((4, HD, TOK), F32),
@@ -690,7 +851,7 @@
             pltpu.VMEM((2, 4, SHARD, D), F32),
             pltpu.VMEM((3, 4, SHARD, D), BF16),
             pltpu.VMEM((3, 3, CHUNK, TOK), BF16),
-            dma((2,)),
+            dma((8,)),
             dma((2,)),
             dma((2,)),
             dma((2, 2)),
@@ -699,31 +860,41 @@
             dma,
             dma((4, 2, 4)),
             dma((4, 2, 4)),
+            dma((4, 3)),
+            dma((4, 2)),
             dma((3, 3)),
             dma((3, 3)),
             dma((2,)),
             dma((2,)),
             dma((4,)),
             dma((4,)),
-            dma((4,)),
+            dma((6,)),
         ],
         compiler_params=pltpu.CompilerParams(
-            collective_id=0, has_side_effects=True, vmem_limit_bytes=48 << 20
+            collective_id=0, has_side_effects=True, vmem_limit_bytes=60 << 20
         ),
     )(
-        down_inputs[0, 0],
-        up_inputs[0, 0],
-        down_cot[0, 0],
-        up_cot[0, 0],
+        down_inputs[0, 0].T,
+        up_inputs[0, 0].T,
+        down_cot[0, 0].T,
+        up_cot[0, 0].T,
         segment_ids,
         patch_rows,
         patch_cols,
         w_qkv.reshape(ROWS, D),
         w_out[0],
     )
+    outs = pl.pallas_call(
+        place,
+        out_shape=shapes,
+        in_specs=[hbm] * 4,
+        out_specs=(hbm,) * 4,
+        scratch_shapes=[pltpu.VMEM(x.shape, BF16) for x in shapes] + [dma((2, 10))],
+        compiler_params=pltpu.CompilerParams(vmem_limit_bytes=60 << 20),
+    )(*outs)
     return (
-        outs[0][None, None],
-        outs[1][None, None],
+        outs[0].T[None, None],
+        outs[1].T[None, None],
         outs[2].reshape(w_qkv.shape),
         outs[3][None],
     )

time: 128 us -> 116 us (0.906)
  the two profiles are of different devices: /device:TPU:3 before, /device:TPU:15 now
where the time goes in v3:
time: 116 us
  Pallas kernels  115 us (99%)
    pallas_call x1, Pallas kernels, per_device(): pl.pallas_call(kernel, out_shape=shapes, in_specs=[hbm] * 9, out_specs=(h...  113 us
    pallas_call x1, Pallas kernels, per_device(): pl.pallas_call(place, out_shape=shapes, in_specs=[hbm] * 4, out_specs=(hb...  2.4 us

profile of v3, /device:TPU:15, one launch (start us, length us, event | category | flops | bytes accessed | tf_op | source)
XLA Modules:
  0.0 115.9 jit_solution(5131414183758529578)
XLA Ops:
  0.6 112.7 %shard_map.120 = (bf16[160,128]{1,0:T(8,128)(2,1)}, bf16[160,128]{1,0:T(8,128)(2,1)}, bf16[480,1280]{1,0:T(8,128)(2,1)}, bf16[160,1280]{1,0:T(8,128)(2,1)}) custom-call(bf16[160,128]{1,0:T(8,128)(2,1)} %bitcast.24, bf16[160,128]{1,0:T(8,128)(2,1)} %bitcast.25, bf16[160,128]{1,0:T(8,128)(2,1)} %bitcast.26, bf16[160,128]{1,0:T(8,128)(2,1)} %bitcast.27, ...), custom_call_target="tpu_custom_call" | custom-call | tf_op jit(solution)/shard_map/pallas_call | solution.py:818
  113.4 2.4 %shard_map.121 = (bf16[160,128]{1,0:T(8,128)(2,1)}, bf16[160,128]{1,0:T(8,128)(2,1)}, bf16[480,1280]{1,0:T(8,128)(2,1)}, bf16[160,1280]{1,0:T(8,128)(2,1)}) custom-call(bf16[160,128]{1,0:T(8,128)(2,1)} %get-tuple-element.12.refs_0_, bf16[160,128]{1,0:T(8,128)(2,1)} %get-tuple-element.13.refs_1_, bf16[480,1280]{1,0:T(8,128)(2,1)} %get-tuple-element.14.refs_2_, ...), custom_call_target="tpu_custom_call" | custom-call | tf_op jit(solution)/shard_map/pallas_call | solution.py:887

commit v4 on v3

--- a/solution.py
+++ b/solution.py
@@ -608,6 +608,7 @@
     await_gather(1, g2, 0, False)
     run_grad_o(g2, 0)
     x1_relay[0]()
+    cot_relay[0]()
 
     @pl.when(has_last)
     def _():
@@ -617,10 +618,9 @@
     def _():
         x2[0] = jnp.zeros_like(x2[0])
 
-    x2_relay[0]()
-    cot_relay[0]()
     both_second(0)
     rs2 = send_partials(1, wq_t, dp2)
+    x2_relay[0]()
     x1_relay[1]()
     reduce_partials(1, rs2, g2)
     g1_own = gather(3, reduced.at[1], g1, p - 1, 0, True)
@@ -632,9 +632,10 @@
         start(g1_own)
         start(g1_other)
 
-    x2_relay[1]()
+    cot_relay[1]()
     x1_relay[2]()
     forward_first(1)
+    x2_relay[1]()
 
     def gradient(slot, j, tick):
         dps, xs = (dp1, x1) if tick == 0 else (dp2, x2)
@@ -663,7 +664,6 @@
     def _():
         g1[...] = jnp.zeros_like(g1)
 
-    cot_relay[1]()
     run_grad_o(g1, 0)
     backward_first(0)
     rs3 = send_partials(2, wq_t, dp1)

time: 116 us -> 117 us (level)
  no operation moved by 1% of the time
where the time goes in v4:
time: 117 us
  Pallas kernels  116 us (99%)
    pallas_call x1, Pallas kernels, per_device(): pl.pallas_call(kernel, out_shape=shapes, in_specs=[hbm] * 9, out_specs=(h...  114 us
    pallas_call x1, Pallas kernels, per_device(): pl.pallas_call(place, out_shape=shapes, in_specs=[hbm] * 4, out_specs=(hb...  2.4 us

profile of v4, /device:TPU:15, one launch (start us, length us, event | category | flops | bytes accessed | tf_op | source)
XLA Modules:
  0.0 116.9 jit_solution(9079355027057919839)
XLA Ops:
  0.6 113.7 %shard_map.120 = (bf16[160,128]{1,0:T(8,128)(2,1)}, bf16[160,128]{1,0:T(8,128)(2,1)}, bf16[480,1280]{1,0:T(8,128)(2,1)}, bf16[160,1280]{1,0:T(8,128)(2,1)}) custom-call(bf16[160,128]{1,0:T(8,128)(2,1)} %bitcast.24, bf16[160,128]{1,0:T(8,128)(2,1)} %bitcast.25, bf16[160,128]{1,0:T(8,128)(2,1)} %bitcast.26, bf16[160,128]{1,0:T(8,128)(2,1)} %bitcast.27, ...), custom_call_target="tpu_custom_call" | custom-call | tf_op jit(solution)/shard_map/pallas_call | solution.py:818
  114.4 2.4 %shard_map.121 = (bf16[160,128]{1,0:T(8,128)(2,1)}, bf16[160,128]{1,0:T(8,128)(2,1)}, bf16[480,1280]{1,0:T(8,128)(2,1)}, bf16[160,1280]{1,0:T(8,128)(2,1)}) custom-call(bf16[160,128]{1,0:T(8,128)(2,1)} %get-tuple-element.12.refs_0_, bf16[160,128]{1,0:T(8,128)(2,1)} %get-tuple-element.13.refs_1_, bf16[480,1280]{1,0:T(8,128)(2,1)} %get-tuple-element.14.refs_2_, ...), custom_call_target="tpu_custom_call" | custom-call | tf_op jit(solution)/shard_map/pallas_call | solution.py:887

commit v5 on v4

--- a/solution.py
+++ b/solution.py
@@ -664,13 +664,13 @@
     def _():
         g1[...] = jnp.zeros_like(g1)
 
+    @pl.when(has_next)
+    def _():
+        g1_forward()
+
     run_grad_o(g1, 0)
     backward_first(0)
     rs3 = send_partials(2, wq_t, dp1)
-
-    @pl.when(has_next)
-    def _():
-        g1_forward()
 
     cot_relay[2]()
     run_grad_o(g2, 1)

time: 117 us -> 122 us (1.043)
  Pallas kernels: 116 us -> 121 us
    pallas_call x1, Pallas kernels: 114 us -> 119 us  [per_device(): pl.pallas_call(kernel, out_shape=shapes, in_specs=[hbm] * 9, out_specs=(h...]
where the time goes in v5:
time: 122 us
  Pallas kernels  121 us (99%)
    pallas_call x1, Pallas kernels, per_device(): pl.pallas_call(kernel, out_shape=shapes, in_specs=[hbm] * 9, out_specs=(h...  119 us

profile of v5, /device:TPU:15, one launch (start us, length us, event | category | flops | bytes accessed | tf_op | source)
XLA Modules:
  0.0 122.1 jit_solution(13258344228531004951)
XLA Ops:
  0.6 118.9 %shard_map.120 = (bf16[160,128]{1,0:T(8,128)(2,1)}, bf16[160,128]{1,0:T(8,128)(2,1)}, bf16[480,1280]{1,0:T(8,128)(2,1)}, bf16[160,1280]{1,0:T(8,128)(2,1)}) custom-call(bf16[160,128]{1,0:T(8,128)(2,1)} %bitcast.24, bf16[160,128]{1,0:T(8,128)(2,1)} %bitcast.25, bf16[160,128]{1,0:T(8,128)(2,1)} %bitcast.26, bf16[160,128]{1,0:T(8,128)(2,1)} %bitcast.27, ...), custom_call_target="tpu_custom_call" | custom-call | tf_op jit(solution)/shard_map/pallas_call | solution.py:818
  119.6 2.4 %shard_map.121 = (bf16[160,128]{1,0:T(8,128)(2,1)}, bf16[160,128]{1,0:T(8,128)(2,1)}, bf16[480,1280]{1,0:T(8,128)(2,1)}, bf16[160,1280]{1,0:T(8,128)(2,1)}) custom-call(bf16[160,128]{1,0:T(8,128)(2,1)} %get-tuple-element.12.refs_0_, bf16[160,128]{1,0:T(8,128)(2,1)} %get-tuple-element.13.refs_1_, bf16[480,1280]{1,0:T(8,128)(2,1)} %get-tuple-element.14.refs_2_, ...), custom_call_target="tpu_custom_call" | custom-call | tf_op jit(solution)/shard_map/pallas_call | solution.py:887
